TPU v7x, 256 devices: a whole 4x4x8 slice. The times are simulated.
256 devices in a mesh: shard: 8 (over y_lo, x), lon: 32 (over z, y_hi, core).
Axes of the slice: x: 4, y: 4 (y_hi: 2, y_lo: 2; y = y_hi * 2 + y_lo), z: 8, core: 2. Of those that a mesh axis runs over, the one named last changes fastest.
Arguments:
- fields: bfloat16 [8, 48, 128, 1024], P('shard', None, 'lon'), may hold values from -6 to 6
- conv_kernel: float32 [3, 3, 1024], replicated, may hold values from -1.8 to 1.8
- gate_weight: bfloat16 [1024, 4096], P(None, 'shard'), may hold values from -0.1875 to 0.1875
- up_weight: bfloat16 [1024, 4096], P(None, 'shard'), may hold values from -0.1875 to 0.1875
- down_weight: bfloat16 [4096, 1024], P('shard'), may hold values from -0.09375 to 0.09375
- cotangent: bfloat16 [8, 48, 128, 1024], P('shard', None, 'lon'), may hold values from -6 to 6
Outputs:
- mlp_out: bfloat16 [8, 48, 128, 1024], P('shard', None, 'lon')
- input_grad: bfloat16 [8, 48, 128, 1024], P('shard', None, 'lon')
- grad_gate: float32 [1024, 4096], P('lon', 'shard')
- grad_up: float32 [1024, 4096], P('lon', 'shard')
- grad_down: float32 [4096, 1024], P('shard', 'lon')
- grad_kernel: float32 [3, 3, 1024], replicated
All inputs are finite; a program needn't handle non-finite values.
Results may differ from a plain program's by a relative error of at most 0.02.
Values may be sent and summed in bfloat16 or wider, within the bound.
A program may use at most 128 MiB of HBM per device.

v0:
```python
import jax
import jax.numpy as jnp
from jax import lax
from jax.sharding import PartitionSpec as P


def extended(array, sides, width):
    for axis, dim in sides:
        size, length = (lax.axis_size(axis), array.shape[dim])
        up = [(i, (i + 1) % size) for i in range(size)]
        down = [(j, i) for i, j in up]
        last = lax.slice_in_dim(array, length - width, length, axis=dim)
        leading = lax.slice_in_dim(array, 0, width, axis=dim)
        before = lax.ppermute(last, axis, up)
        after = lax.ppermute(leading, axis, down)
        array = jnp.concatenate([before, array, after], axis=dim)
    return array


def stencil(widened, kernel):
    height = widened.shape[-3]
    breadth = widened.shape[-2] - 2
    pad_config = [(0, 0)] * (widened.ndim - 3) + [(1, 1), (0, 0), (0, 0)]
    padded = jnp.pad(widened, pad_config)
    summed = jnp.zeros(widened.shape[:-3] + (height, breadth, widened.shape[-1]), jnp.float32)
    for lat_off in range(3):
        for lon_off in range(3):
            summed = (
                summed
                + kernel[lat_off, lon_off]
                * padded[..., lat_off : lat_off + height, lon_off : lon_off + breadth, :]
            )
    return summed


def kernel_terms(grad_field, widened):
    height = widened.shape[-3]
    breadth = widened.shape[-2] - 2
    pad_config = [(0, 0)] * (widened.ndim - 3) + [(1, 1), (0, 0), (0, 0)]
    padded = jnp.pad(widened, pad_config)
    lead_axes = tuple(range(grad_field.ndim - 1))
    listed = []
    for lat_off in range(3):
        for lon_off in range(3):
            window = padded[..., lat_off : lat_off + height, lon_off : lon_off + breadth, :]
            listed.append(jnp.sum(grad_field * window, axis=lead_axes))
    return jnp.stack(listed).reshape(3, 3, grad_field.shape[-1])


def shards(fields, conv_kernel, gate_weight, up_weight, down_weight, cotangent):
    local_shape = fields.shape
    width = local_shape[3]
    samples = lax.axis_size("shard")
    band_tokens = local_shape[1] * local_shape[2]
    total_tokens = samples * local_shape[1] * local_shape[2] * lax.axis_size("lon")
    grad_scale = 1.0 / float(total_tokens) ** 0.5
    flipped = conv_kernel[::-1, ::-1]
    widened = extended(fields, (("lon", 2),), 1).astype(jnp.float32)
    mixed = (fields.astype(jnp.float32) + stencil(widened, conv_kernel)).astype(jnp.bfloat16)
    mixed_all = lax.all_gather(mixed, "shard", axis=0, tiled=True)
    tangent_all = None
    flat_mixed = mixed_all.reshape(-1, width)
    gate = jnp.dot(flat_mixed, gate_weight, preferred_element_type=jnp.float32)
    up_value = jnp.dot(flat_mixed, up_weight, preferred_element_type=jnp.float32)
    sigmas = jax.nn.sigmoid(gate)
    hidden = (gate * sigmas * up_value).astype(jnp.bfloat16)
    hidden_grouped = hidden.reshape(samples, band_tokens, -1)
    product = jnp.einsum(
        "stf,fd->std", hidden_grouped, down_weight, preferred_element_type=jnp.float32
    )
    mlp_out = lax.psum_scatter(
        product.reshape((1 * lax.axis_size("shard"),) + local_shape[1:]).astype(jnp.bfloat16),
        "shard",
        scatter_dimension=0,
        tiled=True,
    )
    tangent_all = lax.all_gather(cotangent, "shard", axis=0, tiled=True)
    flat_tangent = tangent_all.reshape(-1, width)
    dhidden = lax.dot_general(
        flat_tangent, down_weight, (((1,), (1,)), ((), ())), preferred_element_type=jnp.float32
    )
    dgate = (dhidden * up_value * sigmas * (1.0 + gate * (1.0 - sigmas))).astype(jnp.bfloat16)
    dup = (dhidden * gate * sigmas).astype(jnp.bfloat16)
    dgate_grouped = dgate.reshape(samples, band_tokens, -1)
    dup_grouped = dup.reshape(samples, band_tokens, -1)
    product = jnp.einsum(
        "stf,df->std", dgate_grouped, gate_weight, preferred_element_type=jnp.float32
    )
    product = product + jnp.einsum(
        "stf,df->std", dup_grouped, up_weight, preferred_element_type=jnp.float32
    )
    dmixed = lax.psum_scatter(
        product.reshape((1 * lax.axis_size("shard"),) + local_shape[1:]).astype(jnp.bfloat16),
        "shard",
        scatter_dimension=0,
        tiled=True,
    )
    grad_wide = extended(dmixed, (("lon", 2),), 1).astype(jnp.float32)
    dmixed_f = dmixed.astype(jnp.float32)
    input_grad = (dmixed_f + stencil(grad_wide, flipped)).astype(jnp.bfloat16)
    contract_rows = (((0,), (0,)), ((), ()))
    gate_term = (
        lax.dot_general(flat_mixed, dgate, contract_rows, preferred_element_type=jnp.float32)
        * grad_scale
    )
    up_term = (
        lax.dot_general(flat_mixed, dup, contract_rows, preferred_element_type=jnp.float32)
        * grad_scale
    )
    down_term = (
        lax.dot_general(hidden, flat_tangent, contract_rows, preferred_element_type=jnp.float32)
        * grad_scale
    )
    grad_gate, grad_up, grad_down = (
        lax.psum_scatter(
            gate_term.astype(jnp.bfloat16), "lon", scatter_dimension=0, tiled=True
        ).astype(jnp.float32),
        lax.psum_scatter(
            up_term.astype(jnp.bfloat16), "lon", scatter_dimension=0, tiled=True
        ).astype(jnp.float32),
        lax.psum_scatter(
            down_term.astype(jnp.bfloat16), "lon", scatter_dimension=1, tiled=True
        ).astype(jnp.float32),
    )
    kernel_part = kernel_terms(dmixed_f, widened) * grad_scale
    grad_kernel = lax.psum(kernel_part, ("shard", "lon"))
    return (mlp_out, input_grad, grad_gate, grad_up, grad_down, grad_kernel)


def solution(mesh):
    placed = (
        P("shard", None, "lon", None),
        P(),
        P(None, "shard"),
        P(None, "shard"),
        P("shard", None),
        P("shard", None, "lon", None),
    )
    return jax.shard_map(
        shards,
        mesh=mesh,
        in_specs=placed,
        out_specs=(
            P("shard", None, "lon", None),
            P("shard", None, "lon", None),
            P("lon", "shard"),
            P("lon", "shard"),
            P("shard", "lon"),
            P(),
        ),
        check_vma=False,
    )
```

profile of v0, /device:TPU:4, one launch (start us, length us, event | category | flops | bytes accessed | tf_op | source)
XLA Modules:
  0.0 669.2 jit_solution(11417462226580145590)
XLA Ops:
  10.5 8.0 %collective-permute-start.1 = (bf16[1,48,1,1024]{3,1,2,0:T(8,128)(2,1)S(1)}, bf16[1,48,1,1024]{3,1,2,0:T(8,128)(2,1)S(1)}, u32[]{:S(2)}, u32[]{:S(2)}) collective-permute-start(bf16[1,48,1,1024]{3,1,2,0:T(8,128)(2,1)S(1)} %get-tuple-element.39), channel_id=1, source_target_pairs={{1,0},{2,1},{3,2},{4,3},{5,4},{6,5},{7,6},{8,7},{9,8},{10,9},{11,1... | collective-permute-start | bytes 294920 | tf_op jit(solution)/shard_map/ppermute | solution.py:15
  22.5 36.0 %all-gather.5.cloned.1.call-done = bf16[8,48,4,1024]{3,1,2,0:T(8,128)(2,1)} async-done(((bf16[1,48,4,1024]{3,1,2,0:T(8,128)(2,1)}), bf16[8,48,4,1024]{3,1,2,0:T(8,128)(2,1)}) %all-gather.5.cloned.1.call-update) | async-done | bytes 3145744 | tf_op jit(solution)/shard_map/all_gather | solution.py:77
  58.5 6.0 copy.30
  64.6 5.5 reshape.168
  70.1 37.3 %all-gather.3.cloned.1.call-done = bf16[8,48,4,1024]{3,1,2,0:T(8,128)(2,1)} async-done(((bf16[1,48,4,1024]{3,1,2,0:T(8,128)(2,1)}), bf16[8,48,4,1024]{3,1,2,0:T(8,128)(2,1)}) %all-gather.3.cloned.1.call-update) | async-done | bytes 3145744 | tf_op jit(solution)/shard_map/all_gather | solution.py:60
  107.4 6.0 copy.27
  113.4 5.6 reshape.167
  119.0 3.8 fusion.33
  124.8 4.5 multiply_convert_fusion
  133.6 5.2 multiply_convert_fusion.4
  138.8 5.2 multiply_convert_fusion.5
  144.1 3.7 fusion.3
  147.8 3.6 add_convert_fusion
  151.4 5.8 convert_element_type.82
  157.1 4.7 copy.31
  161.9 3.6 dot_general.31
  165.5 4.9 convolution_convert_fusion
  170.5 79.6 %reduce-scatter.14.cloned.1.call-done = bf16[512,32]{0,1:T(8,128)(2,1)} async-done(((bf16[512,1024]{0,1:T(8,128)(2,1)}), bf16[512,32]{0,1:T(8,128)(2,1)}) %reduce-scatter.14.cloned.1.call-update) | async-done | bytes 32784 | tf_op jit(solution)/shard_map/reduce_scatter | solution.py:121
  251.5 116.4 %reduce-scatter.12.cloned.1.call-done = bf16[32,512]{1,0:T(8,128)(2,1)} async-done(((bf16[1024,512]{1,0:T(8,128)(2,1)}), bf16[32,512]{1,0:T(8,128)(2,1)}) %reduce-scatter.12.cloned.1.call-update) | async-done | bytes 32784 | tf_op jit(solution)/shard_map/reduce_scatter | solution.py:118
  369.2 115.8 %reduce-scatter.10.cloned.1.call-done = bf16[32,512]{1,0:T(8,128)(2,1)} async-done(((bf16[1024,512]{1,0:T(8,128)(2,1)}), bf16[32,512]{1,0:T(8,128)(2,1)}) %reduce-scatter.10.cloned.1.call-update) | async-done | bytes 32784 | tf_op jit(solution)/shard_map/reduce_scatter | solution.py:115
  486.4 45.8 %reduce-scatter.8.cloned.1.call-done = bf16[1,48,4,1024]{3,1,2,0:T(8,128)(2,1)} async-done(((bf16[8,48,4,1024]{3,1,2,0:T(8,128)(2,1)}), bf16[1,48,4,1024]{3,1,2,0:T(8,128)(2,1)}) %reduce-scatter.8.cloned.1.call-update) | async-done | bytes 393232 | tf_op jit(solution)/shard_map/reduce_scatter | solution.py:92
  533.3 5.3 collective-permute-start.3
  540.5 42.1 %reduce-scatter.6.cloned.1.call-done = bf16[1,48,4,1024]{3,1,2,0:T(8,128)(2,1)} async-done(((bf16[8,48,4,1024]{3,1,2,0:T(8,128)(2,1)}), bf16[1,48,4,1024]{3,1,2,0:T(8,128)(2,1)}) %reduce-scatter.6.cloned.1.call-update) | async-done | bytes 393232 | tf_op jit(solution)/shard_map/reduce_scatter | solution.py:71
  584.6 75.9 %psum.7 = f32[3,3,1024]{2,1,0:T(4,128)} all-reduce(f32[3,3,1024]{2,1,0:T(4,128)S(1)} %mul.275), channel_id=1, replica_groups=mesh['shard'=8,'lon'=32] {'shard','lon'}, use_global_device_ids=true, to_apply=%region_14.15 | all-reduce | flops 9216 | bytes 73728 | tf_op jit(solution)/shard_map/psum | solution.py:126
  (58 shorter events, 24.5 us)
Async XLA Ops:
  7.2 117.6 %copy-start = (bf16[512,1024]{1,0:T(8,128)(2,1)S(1)}, bf16[512,1024]{1,0:T(8,128)(2,1)}, u32[]{:S(2)}) copy-start(bf16[512,1024]{1,0:T(8,128)(2,1)} %param.10) | copy-start | bytes 3145732
  7.2 13.7 %copy-start.5 = (bf16[1,48,4,1024]{3,2,1,0:T(4,128)(2,1)S(1)}, bf16[1,48,4,1024]{3,2,1,0:T(4,128)(2,1)}, u32[]{:S(2)}) copy-start(bf16[1,48,4,1024]{3,2,1,0:T(4,128)(2,1)} %param.6) | copy-start | bytes 1179652
  7.2 51.3 %all-gather.5.cloned.1.call-start = ((), (), s32[]{:S(2)}) async-start(), calls=%async_computation.7 | async-start | bytes 3538944 | tf_op jit(solution)/shard_map/all_gather | solution.py:77
  9.2 98.1 %all-gather.3.cloned.1.call-start = ((), (), s32[]{:S(2)}) async-start(), calls=%async_computation.5 | async-start | bytes 3538944 | tf_op jit(solution)/shard_map/all_gather | solution.py:60
  10.4 10.3 %collective-permute-start = (bf16[1,48,1,1024]{3,1,2,0:T(8,128)(2,1)S(1)}, bf16[1,48,1,1024]{3,1,2,0:T(8,128)(2,1)S(1)}, u32[]{:S(2)}, u32[]{:S(2)}) collective-permute-start(bf16[1,48,1,1024]{3,1,2,0:T(8,128)(2,1)S(1)} %get-tuple-element.38), channel_id=1, source_target_pairs={{0,1},{1,2},{2,3},{3,4},{4,5},{5,6},{6,7},{7,8},{8,9},{9,10},{10,1... | collective-permute-start | bytes 294920 | tf_op jit(solution)/shard_map/ppermute | solution.py:14
  10.5 10.2 %collective-permute-start.1 = (bf16[1,48,1,1024]{3,1,2,0:T(8,128)(2,1)S(1)}, bf16[1,48,1,1024]{3,1,2,0:T(8,128)(2,1)S(1)}, u32[]{:S(2)}, u32[]{:S(2)}) collective-permute-start(bf16[1,48,1,1024]{3,1,2,0:T(8,128)(2,1)S(1)} %get-tuple-element.39), channel_id=1, source_target_pairs={{1,0},{2,1},{3,2},{4,3},{5,4},{6,5},{7,6},{8,7},{9,8},{10,9},{11,1... | collective-permute-start | bytes 294920 | tf_op jit(solution)/shard_map/ppermute | solution.py:15
  22.3 227.8 %reduce-scatter.14.cloned.1.call-start = ((), (), s32[]{:S(2)}) async-start(), calls=%async_computation.11 | async-start | bytes 1081344 | tf_op jit(solution)/shard_map/reduce_scatter | solution.py:121
  113.4 5.6 copy-start.7
  119.0 3.9 copy-start.2
  119.0 3.9 copy-start.8
  122.9 1.9 copy-start.3
  129.3 1.1 copy-start.4
  133.3 234.6 %reduce-scatter.12.cloned.1.call-start = ((), (), s32[]{:S(2)}) async-start(), calls=%async_computation.10 | async-start | bytes 1081344 | tf_op jit(solution)/shard_map/reduce_scatter | solution.py:118
  138.8 346.3 %reduce-scatter.10.cloned.1.call-start = ((), (), s32[]{:S(2)}) async-start(), calls=%async_computation.9 | async-start | bytes 1081344 | tf_op jit(solution)/shard_map/reduce_scatter | solution.py:115
  144.0 388.2 %reduce-scatter.8.cloned.1.call-start = ((), (), s32[]{:S(2)}) async-start(), calls=%async_computation.8 | async-start | bytes 3538944 | tf_op jit(solution)/shard_map/reduce_scatter | solution.py:92
  144.0 3.7 copy-start.6
  161.8 420.7 %reduce-scatter.6.cloned.1.call-start = ((), (), s32[]{:S(2)}) async-start(), calls=%async_computation.6 | async-start | bytes 3538944 | tf_op jit(solution)/shard_map/reduce_scatter | solution.py:71
  532.2 128.3 %copy-start.1 = (bf16[1,48,4,1024]{3,1,2,0:T(8,128)(2,1)S(1)}, bf16[1,48,4,1024]{3,1,2,0:T(8,128)(2,1)}, u32[]{:S(2)}) copy-start(bf16[1,48,4,1024]{3,1,2,0:T(8,128)(2,1)} %reduce-scatter.8.cloned.1.call-done) | copy-start | bytes 1179652
  533.2 127.3 %collective-permute-start.2 = (bf16[1,48,1,1024]{3,1,2,0:T(8,128)(2,1)S(1)}, bf16[1,48,1,1024]{3,1,2,0:T(8,128)(2,1)S(1)}, u32[]{:S(2)}, u32[]{:S(2)}) collective-permute-start(bf16[1,48,1,1024]{3,1,2,0:T(8,128)(2,1)S(1)} %get-tuple-element.36), channel_id=1, source_target_pairs={{0,1},{1,2},{2,3},{3,4},{4,5},{5,6},{6,7},{7,8},{8,9},{9,10},{10,1... | collective-permute-start | bytes 294920 | tf_op jit(solution)/shard_map/ppermute | solution.py:14
  533.3 127.2 %collective-permute-start.3 = (bf16[1,48,1,1024]{3,1,2,0:T(8,128)(2,1)S(1)}, bf16[1,48,1,1024]{3,1,2,0:T(8,128)(2,1)S(1)}, u32[]{:S(2)}, u32[]{:S(2)}) collective-permute-start(bf16[1,48,1,1024]{3,1,2,0:T(8,128)(2,1)S(1)} %get-tuple-element.37), channel_id=1, source_target_pairs={{1,0},{2,1},{3,2},{4,3},{5,4},{6,5},{7,6},{8,7},{9,8},{10,9},{11,1... | collective-permute-start | bytes 294920 | tf_op jit(solution)/shard_map/ppermute | solution.py:15
Sparse Core Ops, SparseCore 0:
  10.4 48.0 all-gather.4
  60.9 46.4 all-gather.2
  133.4 116.6 reduce-scatter.13
  254.6 113.2 reduce-scatter.11
  371.8 113.1 reduce-scatter.9
  487.6 44.5 reduce-scatter.7
  535.0 47.5 reduce-scatter.5
where the time goes:
time: 673 us; the launch traced here: 669 us
  waiting for transfers between devices  474 us (70%)
  blocking collectives  75.9 us (11%)
  local copies, waits for them, and re-layouts  46.7 us (7%)
  matrix products  35.5 us (5%)
  between operations  14.3 us (2%)
  starting transfers between devices  14.2 us (2%)
  other arithmetic  8.16 us (1%)
    reduce_scatter x1, waiting for transfers between devices, shards(): lax.psum_scatter(up_term.astype(jnp.bfloat16), 'lon', scatter_dimension=0...  116 us
    reduce_scatter x1, waiting for transfers between devices, shards(): lax.psum_scatter(gate_term.astype(jnp.bfloat16), 'lon', scatter_dimension...  116 us
    reduce_scatter x2, waiting for transfers between devices, shards(): lax.psum_scatter(product.reshape((1 * lax.axis_size('shard'),) + local_sh...  87.9 us
    reduce_scatter x1, waiting for transfers between devices, shards(): lax.psum_scatter(down_term.astype(jnp.bfloat16), 'lon', scatter_dimension...  79.6 us
    psum x1, blocking collectives, shards(): grad_kernel = lax.psum(kernel_part, ('shard', 'lon'))  75.9 us
    all_gather x1, waiting for transfers between devices, shards(): mixed_all = lax.all_gather(mixed, 'shard', axis=0, tiled=True)  37.3 us
    all_gather x1, waiting for transfers between devices, shards(): tangent_all = lax.all_gather(cotangent, 'shard', axis=0, tiled=True)  36 us
  transfers between devices with their start and end apart: 11, of which 8 were waited for; matrix products, arithmetic and copies ran while one was open for 9% of the time, Pallas kernels for 0%

commit v1 on v0

v1 whole, which is shorter than its diff:
```python
import jax
import jax.numpy as jnp
from jax import lax
from jax.experimental import pallas as pl
from jax.experimental.pallas import tpu as pltpu
from jax.sharding import PartitionSpec as P

MESH = pl.DeviceIdType.MESH
F32, BF16 = jnp.float32, jnp.bfloat16
NX, NY, NZ, NC = 4, 4, 8, 2
NN = (((1,), (0,)), ((), ()))
NT = (((1,), (1,)), ((), ()))
N_SEM = 128


def mm(a, b, dims=NN):
    return lax.dot_general(a, b, dims, preferred_element_type=F32)


def kernel(
    grad_scale, f_ref, k_ref, wg, wu, wd, t_ref,
    o_out, o_in, o_gg, o_gu, o_gd, o_gk,
    halo, dhalo, wg2, wu2, wd2, mix, cot, hid, dg, du, pb, po, rb3, rb1, ro3, ro1,
    mix_t, cot_t, gb, rc, ry, gz, rz, dm, kp, rk1, rk2, rk3, kf, ssem, rsem,
):
    width, lat = f_ref.shape[2], f_ref.shape[1]
    tok = 4 * lat
    half = tok // 2
    ff = wg.shape[1]
    s, l = lax.axis_index("shard"), lax.axis_index("lon")
    x, yl = lax.rem(s, 4), s // 4
    z, yh, c = l // 4, lax.rem(l // 2, 2), lax.rem(l, 2)
    y = yh * 2 + yl

    def dev(dx=0, dy=0, dz=0, dc=0):
        x2 = lax.rem(x + dx + NX, NX)
        y2 = lax.rem(y + dy + NY, NY)
        z2 = lax.rem(z + dz + NZ, NZ)
        c2 = lax.rem(c + dc, NC)
        return (lax.rem(y2, 2) * 4 + x2, z2 * 4 + (y2 // 2) * 2 + c2)

    lon_up = (s, lax.rem(l + 1, 32))
    lon_down = (s, lax.rem(l + 31, 32))
    squad = [(dx, dc) for dx in range(NX) for dc in range(NC) if (dx, dc) != (0, 0)]
    partners = [dev(dx=dx, dc=dc) for dx, dc in squad]
    partners += [dev(dy=d) for d in range(1, NY)]
    partners += [dev(dz=d) for d in range(1, NZ)]
    partners += [lon_up, lon_down]

    barrier = pltpu.get_barrier_semaphore()
    for p in partners:
        pl.semaphore_signal(barrier, inc=1, device_id=p, device_id_type=MESH)
    pl.semaphore_wait(barrier, len(partners))

    started = []

    def send(src, dst, to):
        i = len(started)
        copy = pltpu.make_async_remote_copy(
            src_ref=src, dst_ref=dst, send_sem=ssem.at[i], recv_sem=rsem.at[i],
            device_id=to, device_id_type=MESH,
        )
        copy.start()
        started.append(copy)
        return copy

    def rows(ref, r0, n):
        return ref.at[pl.ds(r0, n)]

    c_halo = [send(f_ref.at[3], halo.at[0], lon_up), send(f_ref.at[0], halo.at[1], lon_down)]
    slot1, slot2, slot3 = tok, 2 * tok, 3 * tok
    c_cot = [
        send(t_ref, rows(cot, slot1, tok), dev(dx=1)),
        send(t_ref, rows(cot, slot2, tok), dev(dx=-1)),
    ]
    c_w = []
    for own, other in ((wd, wd2), (wg, wg2), (wu, wu2)):
        n = own.shape[0] // 4
        q_up, q_down = rows(own, c * n, n), rows(own, (2 + c) * n, n)
        c_w.append((
            send(q_up, rows(other, c * n, n), dev(dy=1)),
            send(q_down, rows(other, (2 + c) * n, n), dev(dy=-1)),
            other, n,
        ))
    cot[pl.ds(0, tok), :] = t_ref[...]

    row = lax.broadcasted_iota(jnp.int32, (lat, 128), 0)

    def down(v):
        return jnp.where(row == 0, 0.0, pltpu.roll(v, 1, 0))

    def up(v):
        return jnp.where(row == lat - 1, 0.0, pltpu.roll(v, lat - 1, 0))

    def conv(src, edges, flip, store):
        def tile(t, carry):
            cs = pl.ds(pl.multiple_of(t * 128, 128), 128)
            cols = [edges[0, :, cs]] + [src[j, :, cs] for j in range(4)] + [edges[1, :, cs]]
            cols = [v.astype(F32) for v in cols]
            taps = [k_ref[8 - i if flip else i, cs].reshape(1, 128) for i in range(9)]
            for j in range(4):
                a0, a1, a2 = (
                    sum(taps[3 * a + b] * cols[j + b] for b in range(3)) for a in range(3)
                )
                store(j, cs, (cols[j + 1] + a1 + down(a0) + up(a2)).astype(BF16))
            return carry

        lax.fori_loop(0, width // 128, tile, 0)

    for cp in c_halo:
        cp.wait_recv()

    def store_mixed(j, cs, v):
        mix[pl.ds(j * lat, lat), cs] = v

    conv(f_ref, halo, False, store_mixed)
    c_mix = [
        send(rows(mix, 0, tok), rows(mix, slot1, tok), dev(dx=1)),
        send(rows(mix, 0, tok), rows(mix, slot2, tok), dev(dx=-1)),
    ]

    weights = ((wg, wu, wd), (wg2, wu2, wd2))

    def proc(r0, n, h):
        wgr, wur, wdr = weights[h]

        def tile(t, carry):
            cs = pl.ds(pl.multiple_of(t * 256, 256), 256)
            m = mix[pl.ds(r0, n), :]
            gate = mm(m, wgr[:, cs])
            value = mm(m, wur[:, cs])
            dhid = mm(cot[pl.ds(r0, n), :], wdr[cs, :], NT)
            sig = 1.0 / (1.0 + jnp.exp(-gate))
            act = gate * sig
            oc = pl.ds(pl.multiple_of(h * ff + t * 256, 256), 256)
            hid[pl.ds(r0, n), oc] = (act * value).astype(BF16)
            dg[pl.ds(r0, n), oc] = (dhid * value * sig * (1.0 + gate * (1.0 - sig))).astype(BF16)
            du[pl.ds(r0, n), oc] = (dhid * act).astype(BF16)
            return carry

        lax.fori_loop(0, ff // 256, tile, 0)

    def back(r0, n):
        def tile(t, carry):
            cs = pl.ds(pl.multiple_of(t * 256, 256), 256)
            acc = None
            for h in range(2):
                wgr, wur, _ = weights[h]
                hs = pl.ds(h * ff, ff)
                a = mm(dg[pl.ds(r0, n), hs], wgr[cs, :], NT)
                a = a + mm(du[pl.ds(r0, n), hs], wur[cs, :], NT)
                acc = a if acc is None else acc + a
            pb[pl.ds(r0, n), cs] = acc.astype(BF16)
            return carry

        lax.fori_loop(0, width // 256, tile, 0)

    def outp(r0, n):
        def tile(t, carry):
            cs = pl.ds(pl.multiple_of(t * 256, 256), 256)
            acc = mm(hid[pl.ds(r0, n), pl.ds(0, ff)], wd[:, cs])
            acc = acc + mm(hid[pl.ds(r0, n), pl.ds(ff, ff)], wd2[:, cs])
            po[pl.ds(r0, n), cs] = acc.astype(BF16)
            return carry

        lax.fori_loop(0, width // 256, tile, 0)

    def forward(copies, buf):
        copies[0].wait_recv()
        a = send(rows(buf, slot1, half), rows(buf, slot3, half), dev(dx=1))
        copies[1].wait_recv()
        b = send(rows(buf, slot2 + half, half), rows(buf, slot3 + half, half), dev(dx=-1))
        return [a, b]

    def share(i):
        cu, cd, other, n = c_w[i]
        cu.wait_recv()
        cd.wait_recv()
        return [
            send(rows(other, c * n, n), rows(other, c * n, n), dev(dc=1)),
            send(rows(other, (2 + c) * n, n), rows(other, (2 + c) * n, n), dev(dc=1)),
        ]

    proc(0, tok, 0)
    f_cot = forward(c_cot, cot)
    c_share = share(0)
    c_share += share(1)
    f_mix = forward(c_mix, mix)
    proc(tok, 2 * tok, 0)
    c_share += share(2)
    for cp in c_share:
        cp.wait_recv()
    proc(0, 3 * tok, 1)
    for cp in f_cot + f_mix:
        cp.wait_recv()
    proc(slot3, tok, 0)
    proc(slot3, tok, 1)

    def spread3(part, far):
        return [
            send(rows(part, slot3, half), far.at[0], dev(dx=-1)),
            send(rows(part, slot3 + half, half), far.at[1], dev(dx=1)),
        ]

    def spread1(part, near):
        return [
            send(rows(part, slot1 + half, half), near.at[0, pl.ds(half, half)], dev(dx=-1)),
            send(rows(part, slot2, half), near.at[1, pl.ds(0, half)], dev(dx=1)),
        ]

    def merge(part, far, copies, near):
        copies[0].wait_recv()
        r = pl.ds(slot1, half)
        part[r, :] = (part[r, :].astype(F32) + far[0].astype(F32)).astype(BF16)
        a = send(rows(part, slot1, half), near.at[0, pl.ds(0, half)], dev(dx=-1))
        copies[1].wait_recv()
        r = pl.ds(slot2 + half, half)
        part[r, :] = (part[r, :].astype(F32) + far[1].astype(F32)).astype(BF16)
        b = send(rows(part, slot2 + half, half), near.at[1, pl.ds(half, half)], dev(dx=1))
        return [a, b]

    back(slot3, tok)
    c_b3 = spread3(pb, rb3)
    back(tok, 2 * tok)
    c_b1 = spread1(pb, rb1)
    outp(slot3, tok)
    c_o3 = spread3(po, ro3)
    outp(tok, 2 * tok)
    c_o1 = spread1(po, ro1)

    def transpose(src, dst):
        for pair in range(2):
            for b in range(width // 128):
                v = src[pl.ds(pair * 2 * tok, 2 * tok), pl.ds(b * 128, 128)].T
                for q in range(4):
                    dst[q % 2, q // 2, pl.ds(b * 32, 32), pl.ds(pair * 2 * tok, 2 * tok)] = v[
                        q * 32 : q * 32 + 32
                    ]

    def weight_grad(g, lhs, rhs):
        for cc in (1 - c, c):
            for h in range(2):
                yl2 = yl if h == 0 else 1 - yl

                def tile(t, carry, cc=cc, h=h, yl2=yl2):
                    yh2, n2 = t // 2, lax.rem(t, 2)
                    cs = pl.ds(pl.multiple_of(h * ff + n2 * 256, 256), 256)
                    v = mm(lhs[cc, yh2], rhs[:, cs]) * grad_scale
                    gb[g, cc, yh2 * 2 + yl2, :, pl.ds(pl.multiple_of(n2 * 256, 256), 256)] = (
                        v.astype(BF16)
                    )
                    return carry

                lax.fori_loop(0, 4, tile, 0)
            if cc is not c:
                cp = send(gb.at[g, cc], rc.at[g], dev(dc=1))
        return cp

    def add_core(g, cp):
        cp.wait_recv()

        def tile(t, carry):
            gb[g, c, t] = (gb[g, c, t].astype(F32) + rc[g, t].astype(F32)).astype(BF16)
            return carry

        lax.fori_loop(0, NY, tile, 0)
        return [send(gb.at[g, c, lax.rem(y + d, NY)], ry.at[g, d - 1], dev(dy=d)) for d in (1, 3, 2)]

    def add_y(g, cps):
        for cp in cps:
            cp.wait_recv()
        v = gb[g, c, y].astype(F32)
        for d in range(NY - 1):
            v = v + ry[g, d].astype(F32)
        gz[g] = v.astype(BF16).reshape(NZ, 32, ff)
        return [
            send(gz.at[g, lax.rem(z + d, NZ)], rz.at[g, d - 1], dev(dz=d))
            for d in (4, 3, 5, 2, 6, 1, 7)
        ]

    def add_z(g, cps, out):
        for cp in cps:
            cp.wait_recv()
        v = gz[g, z].astype(F32)
        for d in range(NZ - 1):
            v = v + rz[g, d].astype(F32)
        out[...] = v

    transpose(mix, mix_t)
    g0 = weight_grad(0, mix_t, dg)
    c_b1 += merge(pb, rb3, c_b3, rb1)
    g1 = weight_grad(1, mix_t, du)
    y0 = add_core(0, g0)
    c_o1 += merge(po, ro3, c_o3, ro1)
    transpose(cot, cot_t)
    g2 = weight_grad(2, cot_t, hid)
    y1 = add_core(1, g1)
    back(0, tok)
    outp(0, tok)
    y2 = add_core(2, g2)

    def total(part, near, copies, store):
        for cp in copies:
            cp.wait_recv()
        for j in range(4):
            r = pl.ds(j * lat, lat)
            v = part[r, :].astype(F32) + near[0, r, :].astype(F32) + near[1, r, :].astype(F32)
            store(j, v.astype(BF16))

    def store_dm(j, v):
        dm[j] = v

    total(pb, rb1, c_b1, store_dm)
    c_dh = [send(dm.at[3], dhalo.at[0], lon_up), send(dm.at[0], dhalo.at[1], lon_down)]

    def kernel_tile(e, carry):
        cs = pl.ds(pl.multiple_of(e * 128, 128), 128)
        cols = [halo[0, :, cs]] + [f_ref[j, :, cs] for j in range(4)] + [halo[1, :, cs]]
        cols = [v.astype(F32) for v in cols]
        sums = [None] * 9
        for j in range(4):
            d = dm[j, :, cs].astype(F32)
            for a, v in enumerate((up(d), d, down(d))):
                for b in range(3):
                    p = v * cols[j + b]
                    i = 3 * a + b
                    sums[i] = p if sums[i] is None else sums[i] + p
        for i in range(9):
            kp[e, pl.ds(i, 1), :] = jnp.sum(sums[i], axis=0, keepdims=True) * grad_scale
        return carry

    kp[...] = jnp.zeros(kp.shape, F32)
    lax.fori_loop(0, NX * NC, kernel_tile, 0)
    me = 2 * x + c
    c_k = []
    for i, (dx, dc) in enumerate(squad):
        to = 2 * lax.rem(x + dx, NX) + lax.rem(c + dc, NC)
        c_k.append(send(kp.at[to], rk1.at[i], dev(dx=dx, dc=dc)))

    z0 = add_y(0, y0)

    for cp in c_k:
        cp.wait_recv()
    v = kp[me]
    for i in range(len(squad)):
        v = v + rk1[i]
    rk2[y] = v
    c_k = [send(rk2.at[y], rk2.at[y], dev(dy=d)) for d in range(1, NY)]

    for cp in c_dh:
        cp.wait_recv()

    def store_in(j, cs, v):
        o_in[j, :, cs] = v

    conv(dm, dhalo, True, store_in)

    for cp in c_k:
        cp.wait_recv()
    rk3[z] = rk2[0] + rk2[1] + rk2[2] + rk2[3]
    c_k = [send(rk3.at[z], rk3.at[z], dev(dz=d)) for d in range(1, NZ)]

    z1 = add_y(1, y1)

    for cp in c_k:
        cp.wait_recv()
    v = rk3[0]
    for i in range(1, NZ):
        v = v + rk3[i]
    kf[me] = v
    c_k = [send(kf.at[me], kf.at[me], dev(dx=dx, dc=dc)) for dx, dc in squad]

    def store_out(j, v):
        o_out[pl.ds(j * lat, lat), :] = v

    total(po, ro1, c_o1, store_out)
    z2 = add_y(2, y2)
    add_z(0, z0, o_gg)
    add_z(1, z1, o_gu)
    for cp in c_k:
        cp.wait_recv()
    for e in range(NX * NC):
        o_gk[:, pl.ds(e * 128, 128)] = kf[e]
    add_z(2, z2, o_gd)
    for cp in started:
        cp.wait_send()


def shards(fields, conv_kernel, gate_weight, up_weight, down_weight, cotangent):
    _, lat, lon, width = fields.shape
    ff = gate_weight.shape[1]
    tok = lat * lon
    total_tokens = tok * lax.axis_size("shard") * lax.axis_size("lon")
    grad_scale = 1.0 / float(total_tokens) ** 0.5
    field_cols = fields[0].transpose(1, 0, 2)
    tangent = cotangent[0].transpose(1, 0, 2).reshape(tok, width)
    taps = conv_kernel.reshape(9, width)
    rows_d = width // 32
    vmem = lambda *shape, dtype=BF16: pltpu.VMEM(shape, dtype)
    call = pl.pallas_call(
        lambda *refs: kernel(grad_scale, *refs),
        name="swiglu_block",
        out_shape=[
            jax.ShapeDtypeStruct((tok, width), BF16),
            jax.ShapeDtypeStruct((lon, lat, width), BF16),
            jax.ShapeDtypeStruct((rows_d, ff), F32),
            jax.ShapeDtypeStruct((rows_d, ff), F32),
            jax.ShapeDtypeStruct((rows_d, ff), F32),
            jax.ShapeDtypeStruct((16, width), F32),
        ],
        in_specs=[pl.BlockSpec(memory_space=pltpu.VMEM)] * 6,
        out_specs=[pl.BlockSpec(memory_space=pltpu.VMEM)] * 6,
        scratch_shapes=[
            vmem(2, lat, width),
            vmem(2, lat, width),
            vmem(width, ff),
            vmem(width, ff),
            vmem(ff, width),
            vmem(4 * tok, width),
            vmem(4 * tok, width),
            vmem(4 * tok, 2 * ff),
            vmem(4 * tok, 2 * ff),
            vmem(4 * tok, 2 * ff),
            vmem(4 * tok, width),
            vmem(4 * tok, width),
            vmem(2, tok // 2, width),
            vmem(2, tok, width),
            vmem(2, tok // 2, width),
            vmem(2, tok, width),
            vmem(2, 2, width // 4, 4 * tok),
            vmem(2, 2, width // 4, 4 * tok),
            vmem(3, 2, NY, width // 4, ff),
            vmem(3, NY, width // 4, ff),
            vmem(3, NY - 1, width // 4, ff),
            vmem(3, NZ, 32, ff),
            vmem(3, NZ - 1, 32, ff),
            vmem(lon, lat, width),
            vmem(8, 16, width // 8, dtype=F32),
            vmem(7, 16, width // 8, dtype=F32),
            vmem(NY, 16, width // 8, dtype=F32),
            vmem(NZ, 16, width // 8, dtype=F32),
            vmem(8, 16, width // 8, dtype=F32),
            pltpu.SemaphoreType.DMA((N_SEM,)),
            pltpu.SemaphoreType.DMA((N_SEM,)),
        ],
        compiler_params=pltpu.CompilerParams(
            collective_id=0, has_side_effects=True, vmem_limit_bytes=60 * 2**20
        ),
        cost_estimate=pl.CostEstimate(flops=14_500_000_000, bytes_accessed=6_000_000, transcendentals=800_000),
    )
    out, in_grad, gg, gu, gd, gk = call(
        field_cols, taps, gate_weight, up_weight, down_weight, tangent
    )

    def placed(v):
        return v.reshape(lon, lat, width).transpose(1, 0, 2)[None]

    return placed(out), placed(in_grad), gg, gu, gd.T, gk[:9].reshape(3, 3, width)


def solution(mesh):
    placed = (
        P("shard", None, "lon", None),
        P(),
        P(None, "shard"),
        P(None, "shard"),
        P("shard", None),
        P("shard", None, "lon", None),
    )
    return jax.shard_map(
        shards,
        mesh=mesh,
        in_specs=placed,
        out_specs=(
            P("shard", None, "lon", None),
            P("shard", None, "lon", None),
            P("lon", "shard"),
            P("lon", "shard"),
            P("shard", "lon"),
            P(),
        ),
        check_vma=False,
    )
```

time: 673 us -> 127 us (0.19)
  waiting for transfers between devices: 474 us -> 0 us
  Pallas kernels: 0 us -> 113 us
  blocking collectives: 75.9 us -> 0 us
  local copies, waits for them, and re-layouts: 46.7 us -> 10.6 us
  matrix products: 35.5 us -> 0 us
  starting transfers between devices: 14.2 us -> 0 us
  between operations: 14.3 us -> 0.66 us
  other arithmetic: 8.16 us -> 0 us
    reduce_scatter x5 -> x0, waiting for transfers between devices: 400 us -> none  [the longest x1 116 us: shards(): lax.psum_scatter(up_term.astype(jnp.bfloat16), 'lon', scatter_dimension=0...]
    pallas_call x0 -> x1, Pallas kernels: none -> 113 us  [shards(): call(field_cols, taps, gate_weight, up_weight, down_weight, tangent)]
    psum x1 -> x0, blocking collectives: 75.9 us -> none  [shards(): grad_kernel = lax.psum(kernel_part, ('shard', 'lon'))]
    all_gather x2 -> x0, waiting for transfers between devices: 73.3 us -> none  [the longest x1 37.3 us: shards(): mixed_all = lax.all_gather(mixed, 'shard', axis=0, tiled=True)]
    dot_general x9 -> x0, matrix products: 35.5 us -> none  [the longest x1 5.16 us: shards(): lax.dot_general(flat_mixed, dgate, contract_rows, preferred_element_type=...]
    ppermute x4 -> x0, starting transfers between devices: 13.5 us -> none  [the longest x2 13.3 us: extended(): after = lax.ppermute(leading, axis, down)]
    all_gather x2 -> x0, local copies, waits for them, and re-layouts: 12.1 us -> none  [the longest x1 6.03 us: shards(): tangent_all = lax.all_gather(cotangent, 'shard', axis=0, tiled=True)]
    convert_element_type x2 -> x0, local copies, waits for them, and re-layouts: 10.4 us -> none  [shards(): product.reshape((1 * lax.axis_size('shard'),) + local_shape[1:])]
  transfers between devices with their start and end apart: 11 -> 0, of which waited for: 8 -> 0; matrix products, arithmetic and copies ran while one was open for 9% -> 0% of each run, Pallas kernels for 0% -> 0%
where the time goes in v1:
time: 127 us; the launch traced here: 125 us
  Pallas kernels  113 us (89%)
  local copies, waits for them, and re-layouts  10.6 us (8%)
    pallas_call x1, Pallas kernels, shards(): call(field_cols, taps, gate_weight, up_weight, down_weight, tangent)  113 us
    unnamed x17, local copies, waits for them, and re-layouts  5.53 us

profile of v1, /device:TPU:4, one launch (start us, length us, event | category | flops | bytes accessed | tf_op | source)
XLA Modules:
  0.0 124.6 jit_solution(16041094779393957656)
XLA Ops:
  0.6 1.4 %reshape.24.refs_1_ = f32[9,1024]{1,0:T(8,128)} reshape(f32[3,3,1024]{2,1,0:T(4,128)} %param.7) | data formatting | bytes 73728 | tf_op jit(solution)/shard_map/reshape | solution.py:397
  2.1 0.0 copy-start
  2.1 1.9 %copy.19 = bf16[1,48,4,1024]{3,1,2,0:T(8,128)(2,1)} copy(bf16[1,48,4,1024]{3,2,1,0:T(4,128)(2,1)} %param.6) | data formatting | bytes 786432 | tf_op args[0]
  4.0 0.0 copy-done
  4.0 0.9 copy.13
  4.9 113.4 %swiglu_block.1 = (bf16[192,1024]{1,0:T(8,128)(2,1)}, bf16[4,48,1024]{2,1,0:T(8,128)(2,1)}, f32[32,512]{1,0:T(8,128)}, f32[32,512]{1,0:T(8,128)}, f32[32,512]{1,0:T(8,128)}, /*index=5*/f32[16,1024]{1,0:T(8,128)}) custom-call(bf16[4,48,1024]{2,1,0:T(8,128)(2,1)} %bitcast.24, f32[9,1024]{1,0:T(8,128)} %reshape.24.refs_1_, bf16[1024,512]{1,0:T(8,128)(2,1)} %refs_2_.1, ...), custom_call_target="tpu_custom_call" | custom-call | flops 14499999744 | bytes 6000000 | tf_op jit(solution)/shard_map/swiglu_block/pallas_call | solution.py:451
  118.2 0.0 copy-start.1
  118.2 2.1 %copy.18 = bf16[4,48,1024]{2,0,1:T(4,128)(2,1)} copy(bf16[4,48,1024]{2,1,0:T(8,128)(2,1)} %bitcast.23) | data formatting | bytes 786432 | tf_op jit(solution)/shard_map/reshape | solution.py:456
  120.3 0.0 copy-done.1
  120.3 0.0 copy-start.2
  120.3 1.1 copy.15
  121.4 0.0 copy-done.2
  121.4 0.0 copy-start.5
  121.4 0.6 reshape.27
  122.0 0.2 copy-done.5
  122.2 0.0 copy-start.4
  122.2 0.6 copy.23
  122.9 0.2 copy-done.4
  123.1 0.0 copy-start.3
  123.1 0.6 copy.24
  123.7 0.2 copy-done.3
  124.0 0.6 copy.25
Async XLA Ops:
  2.1 1.9 %copy-start = (bf16[1,48,4,1024]{3,2,1,0:T(4,128)(2,1)S(1)}, bf16[1,48,4,1024]{3,2,1,0:T(4,128)(2,1)}, u32[]{:S(2)}) copy-start(bf16[1,48,4,1024]{3,2,1,0:T(4,128)(2,1)} %param.11) | copy-start | bytes 1179652
  118.2 2.1 %copy-start.1 = (bf16[4,48,1024]{2,1,0:T(8,128)(2,1)S(1)}, bf16[4,48,1024]{2,1,0:T(8,128)(2,1)}, u32[]{:S(2)}) copy-start(bf16[4,48,1024]{2,1,0:T(8,128)(2,1)} %get-tuple-element.13) | copy-start | bytes 1179652
  120.3 1.1 copy-start.2
  121.4 0.8 copy-start.5
  122.2 0.9 copy-start.4
  123.1 0.9 copy-start.3

commit v2 on v1

v2 whole, which is shorter than its diff:
```python
import jax
import jax.numpy as jnp
from jax import lax
from jax.experimental import pallas as pl
from jax.experimental.pallas import tpu as pltpu
from jax.sharding import PartitionSpec as P

MESH = pl.DeviceIdType.MESH
F32, BF16 = jnp.float32, jnp.bfloat16
NX, NY, NZ, NC = 4, 4, 8, 2
NN = (((1,), (0,)), ((), ()))
NT = (((1,), (1,)), ((), ()))
N_SEM = 128


def mm(a, b, dims=NN):
    return lax.dot_general(a, b, dims, preferred_element_type=F32)


def kernel(
    grad_scale, f_in, k_ref, wg_in, wu_in, wd_in, t_in,
    o_out, o_in, o_gg, o_gu, o_gd, o_gk,
    f_raw, t_raw, f_ref, wg, wu, wd, halo, dhalo, wg2, wu2, wd2, mix, cot, hid, dg, du, pb, po, rb3, rb1, ro3, ro1,
    dh, mix_t, cot_t, gb, rc, ry2, ry1, gz, rz, zr, gy, rzy, dm, kp, rk1, rk2, rk3, kf, ssem, rsem, lsem,
):
    width, lat = f_ref.shape[2], f_ref.shape[1]
    local = [
        pltpu.make_async_copy(src, dst, lsem.at[i])
        for i, (src, dst) in enumerate((
            (f_in, f_raw), (t_in, t_raw), (wd_in, wd), (wg_in, wg), (wu_in, wu),
        ))
    ]
    for cp in local:
        cp.start()
    tok = 4 * lat
    half = tok // 2
    ff = wg.shape[1]
    s, l = lax.axis_index("shard"), lax.axis_index("lon")
    x, yl = lax.rem(s, 4), s // 4
    z, yh, c = l // 4, lax.rem(l // 2, 2), lax.rem(l, 2)
    y = yh * 2 + yl

    def dev(dx=0, dy=0, dz=0, dc=0):
        x2 = lax.rem(x + dx + NX, NX)
        y2 = lax.rem(y + dy + NY, NY)
        z2 = lax.rem(z + dz + NZ, NZ)
        c2 = lax.rem(c + dc, NC)
        return (lax.rem(y2, 2) * 4 + x2, z2 * 4 + (y2 // 2) * 2 + c2)

    lon_up = (s, lax.rem(l + 1, 32))
    lon_down = (s, lax.rem(l + 31, 32))
    squad = [(dx, dc) for dx in range(NX) for dc in range(NC) if (dx, dc) != (0, 0)]
    partners = [dev(dx=dx, dc=dc) for dx, dc in squad]
    partners += [dev(dy=d) for d in range(1, NY)]
    partners += [dev(dz=d) for d in range(1, NZ)]
    partners += [lon_up, lon_down]

    barrier = pltpu.get_barrier_semaphore()
    for p in partners:
        pl.semaphore_signal(barrier, inc=1, device_id=p, device_id_type=MESH)
    pl.semaphore_wait(barrier, len(partners))

    started = []

    def send(src, dst, to):
        i = len(started)
        copy = pltpu.make_async_remote_copy(
            src_ref=src, dst_ref=dst, send_sem=ssem.at[i], recv_sem=rsem.at[i],
            device_id=to, device_id_type=MESH,
        )
        copy.start()
        started.append(copy)
        return copy

    def rows(ref, r0, n):
        return ref.at[pl.ds(r0, n)]

    local[0].wait()
    f_ref[...] = jnp.swapaxes(f_raw[...], 0, 1)
    c_halo = [send(f_ref.at[3], halo.at[0], lon_up), send(f_ref.at[0], halo.at[1], lon_down)]
    slot1, slot2, slot3 = tok, 2 * tok, 3 * tok
    local[1].wait()
    cot[pl.ds(0, tok), :] = jnp.swapaxes(t_raw[...], 0, 1).reshape(tok, width)
    c_cot = [
        send(rows(cot, 0, tok), rows(cot, slot1, tok), dev(dx=1)),
        send(rows(cot, 0, tok), rows(cot, slot2, tok), dev(dx=-1)),
    ]
    c_w = []
    for i, (own, other) in enumerate(((wd, wd2), (wg, wg2), (wu, wu2))):
        local[2 + i].wait()
        n = own.shape[0] // 4
        q_up, q_down = rows(own, c * n, n), rows(own, (2 + c) * n, n)
        c_w.append((
            send(q_up, rows(other, c * n, n), dev(dy=1)),
            send(q_down, rows(other, (2 + c) * n, n), dev(dy=-1)),
            other, n,
        ))

    row = lax.broadcasted_iota(jnp.int32, (lat, 128), 0)

    def down(v):
        return jnp.where(row == 0, 0.0, pltpu.roll(v, 1, 0))

    def up(v):
        return jnp.where(row == lat - 1, 0.0, pltpu.roll(v, lat - 1, 0))

    def conv(src, edges, flip, store):
        for t in range(width // 128):
            cs = pl.ds(t * 128, 128)
            cols = [edges[0, :, cs]] + [src[j, :, cs] for j in range(4)] + [edges[1, :, cs]]
            cols = [v.astype(F32) for v in cols]
            taps = [
                k_ref[2 - a if flip else a, 2 - b if flip else b, cs].reshape(1, 128)
                for a in range(3) for b in range(3)
            ]
            for j in range(4):
                a0, a1, a2 = (
                    sum(taps[3 * a + b] * cols[j + b] for b in range(3)) for a in range(3)
                )
                store(j, cs, (cols[j + 1] + a1 + down(a0) + up(a2)).astype(BF16))

    for cp in c_halo:
        cp.wait_recv()

    def store_mixed(j, cs, v):
        mix[pl.ds(j * lat, lat), cs] = v

    conv(f_ref, halo, False, store_mixed)
    c_mix = [
        send(rows(mix, 0, tok), rows(mix, slot1, tok), dev(dx=1)),
        send(rows(mix, 0, tok), rows(mix, slot2, tok), dev(dx=-1)),
    ]

    def transpose(src, dst, pair):
        r = pl.ds(pair * 2 * tok, 2 * tok)
        for b in range(width // 128):
            v = src[r, pl.ds(b * 128, 128)].T
            for q in range(4):
                dst[q % 2, pl.ds(q // 2 * 256 + b * 32, 32), r] = v[q * 32 : q * 32 + 32]

    weights = ((wg, wu, wd), (wg2, wu2, wd2))

    def proc_d(r0, n, h):
        wdr = weights[h][2]
        dh[pl.ds(r0, n), pl.ds(h * ff, ff)] = mm(cot[pl.ds(r0, n), :], wdr[...], NT)

    def proc_g(r0, n, h):
        wgr, wur, _ = weights[h]
        r = pl.ds(r0, n)
        for t in range(ff // 256):
            cs = pl.ds(t * 256, 256)
            oc = pl.ds(h * ff + t * 256, 256)
            gate = mm(mix[r, :], wgr[:, cs])
            value = mm(mix[r, :], wur[:, cs])
            dhid = dh[r, oc]
            sig = 1.0 / (1.0 + jnp.exp(-gate))
            act = gate * sig
            hid[r, oc] = (act * value).astype(BF16)
            dg[r, oc] = (dhid * value * sig * (1.0 + gate * (1.0 - sig))).astype(BF16)
            du[r, oc] = (dhid * act).astype(BF16)

    def back(r0, n):
        r = pl.ds(r0, n)
        for t in range(width // 512):
            cs = pl.ds(t * 512, 512)
            acc = None
            for h in range(2):
                wgr, wur, _ = weights[h]
                hs = pl.ds(h * ff, ff)
                a = mm(dg[r, hs], wgr[cs, :], NT) + mm(du[r, hs], wur[cs, :], NT)
                acc = a if acc is None else acc + a
            pb[r, cs] = acc.astype(BF16)

    def outp(r0, n):
        r = pl.ds(r0, n)
        for t in range(width // 512):
            cs = pl.ds(t * 512, 512)
            acc = mm(hid[r, pl.ds(0, ff)], wd[:, cs]) + mm(hid[r, pl.ds(ff, ff)], wd2[:, cs])
            po[r, cs] = acc.astype(BF16)

    def forward(copies, buf):
        copies[0].wait_recv()
        a = send(rows(buf, slot1, half), rows(buf, slot3, half), dev(dx=1))
        copies[1].wait_recv()
        b = send(rows(buf, slot2 + half, half), rows(buf, slot3 + half, half), dev(dx=-1))
        return [a, b]

    def share(i):
        cu, cd, other, n = c_w[i]
        cu.wait_recv()
        cd.wait_recv()
        return [
            send(rows(other, c * n, n), rows(other, c * n, n), dev(dc=1)),
            send(rows(other, (2 + c) * n, n), rows(other, (2 + c) * n, n), dev(dc=1)),
        ]

    proc_d(0, tok, 0)
    proc_g(0, tok, 0)
    c_share = share(0)
    f_cot = forward(c_cot, cot)
    proc_d(slot1, 2 * tok, 0)
    c_share += share(1)
    for cp in c_share:
        cp.wait_recv()
    transpose(cot, cot_t, 0)
    c_share2 = share(2)
    f_mix = forward(c_mix, mix)
    proc_d(0, 3 * tok, 1)
    for cp in c_share2:
        cp.wait_recv()
    proc_g(0, tok, 1)
    proc_g(slot1, 2 * tok, 0)
    proc_g(slot1, 2 * tok, 1)
    transpose(mix, mix_t, 0)
    back(0, 3 * tok)
    outp(0, 3 * tok)
    for cp in f_cot:
        cp.wait_recv()
    proc_d(slot3, tok, 0)
    proc_d(slot3, tok, 1)
    transpose(cot, cot_t, 1)
    for cp in f_mix:
        cp.wait_recv()

    def spread3(part, far):
        return [
            send(rows(part, slot3, half), far.at[0], dev(dx=-1)),
            send(rows(part, slot3 + half, half), far.at[1], dev(dx=1)),
        ]

    def spread1(part, near):
        return [
            send(rows(part, slot1 + half, half), near.at[0, pl.ds(half, half)], dev(dx=-1)),
            send(rows(part, slot2, half), near.at[1, pl.ds(0, half)], dev(dx=1)),
        ]

    def merge(part, far, copies, near):
        copies[0].wait_recv()
        r = pl.ds(slot1, half)
        part[r, :] = (part[r, :].astype(F32) + far[0].astype(F32)).astype(BF16)
        a = send(rows(part, slot1, half), near.at[0, pl.ds(0, half)], dev(dx=-1))
        copies[1].wait_recv()
        r = pl.ds(slot2 + half, half)
        part[r, :] = (part[r, :].astype(F32) + far[1].astype(F32)).astype(BF16)
        b = send(rows(part, slot2 + half, half), near.at[1, pl.ds(half, half)], dev(dx=1))
        return [a, b]

    def weight_grad(g, lhs, rhs):
        cp = None
        for cc in (1 - c, c):
            for h in range(2):
                yl2 = yl if h == 0 else 1 - yl
                v = mm(lhs[cc], rhs[:, pl.ds(h * ff, ff)]) * grad_scale
                for yh2 in range(2):
                    gb[g, cc, yh2 * 2 + yl2] = v[yh2 * 256 : yh2 * 256 + 256].astype(BF16)
            if cp is None:
                cp = send(gb.at[g, cc], rc.at[g], dev(dc=1))
        return cp

    def add_core(g, cp):
        cp.wait_recv()
        for t in range(NY):
            gb[g, c, t] = (gb[g, c, t].astype(F32) + rc[g, t].astype(F32)).astype(BF16)

    yup, ydown, yfar = lax.rem(y + 1, NY), lax.rem(y + 3, NY), lax.rem(y + 2, NY)
    n_y = gb.shape[3]
    h_y = n_y // 2

    def y_first(g):
        lo, hi = pl.ds(0, h_y), pl.ds(h_y, h_y)
        far = [
            send(gb.at[g, c, yfar, lo], ry2.at[g, 0], dev(dy=-1)),
            send(gb.at[g, c, yfar, hi], ry2.at[g, 1], dev(dy=1)),
        ]
        near = [
            send(gb.at[g, c, ydown, hi], ry1.at[g, 0, hi], dev(dy=-1)),
            send(gb.at[g, c, yup, lo], ry1.at[g, 1, lo], dev(dy=1)),
        ]
        return far, near

    def y_merge(g, cps):
        far, near = cps
        lo, hi = pl.ds(0, h_y), pl.ds(h_y, h_y)
        far[0].wait_recv()
        gb[g, c, ydown, lo] = (gb[g, c, ydown, lo].astype(F32) + ry2[g, 0].astype(F32)).astype(BF16)
        near.append(send(gb.at[g, c, ydown, lo], ry1.at[g, 0, lo], dev(dy=-1)))
        far[1].wait_recv()
        gb[g, c, yup, hi] = (gb[g, c, yup, hi].astype(F32) + ry2[g, 1].astype(F32)).astype(BF16)
        near.append(send(gb.at[g, c, yup, hi], ry1.at[g, 1, hi], dev(dy=1)))
        return near

    def y_last(g, near):
        for cp in near:
            cp.wait_recv()
        v = gb[g, c, y].astype(F32) + ry1[g, 0].astype(F32) + ry1[g, 1].astype(F32)
        gz[g] = v.astype(BF16).reshape(NZ, 32, ff)
        return [
            send(gz.at[g, lax.rem(z + d, NZ)], rz.at[g, d - 1], dev(dz=d))
            for d in (4, 3, 5, 2, 6, 1, 7)
        ]

    def z_last(g, cps, out):
        for cp in cps:
            cp.wait_recv()
        v = gz[g, z].astype(F32)
        for d in range(NZ - 1):
            v = v + rz[g, d].astype(F32)
        out[...] = v

    def stripe(d, r0, n):
        return pl.ds(pl.multiple_of(lax.rem(z + d + NZ, NZ) * 32 + r0, 16), n)

    def z_step(k, cps):
        new = []
        for way, sign in ((0, 1), (1, -1)):
            if k == 1:
                st = stripe(4, way * 16, 16)
                new.append(send(gb.at[2, c, :, st], zr.at[way, 0, :, pl.ds(way * 16, 16)], dev(dz=sign)))
                continue
            cps[way].wait_recv()
            if k == 2:
                st, r = stripe(3 * sign, way * 16, 16), pl.ds(way * 16, 16)
            else:
                st, r = stripe((5 - k) * sign, 0, 32), pl.ds(0, 32)
            gb[2, c, :, st] = (gb[2, c, :, st].astype(F32) + zr[way, k - 2, :, r].astype(F32)).astype(BF16)
            st = stripe((5 - k) * sign, 0, 32)
            new.append(send(gb.at[2, c, :, st], zr.at[way, k - 1], dev(dz=sign)))
        return new

    def z_done(cps):
        for cp in cps:
            cp.wait_recv()
        st = stripe(0, 0, 32)
        v = gb[2, c, :, st].astype(F32) + zr[0, 3].astype(F32) + zr[1, 3].astype(F32)
        gy[...] = v.astype(BF16)
        return [
            send(gy.at[lax.rem(y + d, NY)], rzy.at[d - 1], dev(dy=d)) for d in range(1, NY)
        ]

    def zy_last(cps, out):
        for cp in cps:
            cp.wait_recv()
        v = gy[y].astype(F32)
        for d in range(NY - 1):
            v = v + rzy[d].astype(F32)
        out[...] = v

    def total(part, near, copies, store):
        for cp in copies:
            cp.wait_recv()
        for j in range(4):
            r = pl.ds(j * lat, lat)
            v = part[r, :].astype(F32) + near[0, r, :].astype(F32) + near[1, r, :].astype(F32)
            store(j, v.astype(BF16))

    def store_dm(j, v):
        dm[j] = v

    def kernel_tile(e):
        cs = pl.ds(e * 128, 128)
        cols = [halo[0, :, cs]] + [f_ref[j, :, cs] for j in range(4)] + [halo[1, :, cs]]
        cols = [v.astype(F32) for v in cols]
        sums = [None] * 9
        for j in range(4):
            d = dm[j, :, cs].astype(F32)
            for a, v in enumerate((up(d), d, down(d))):
                for b in range(3):
                    p = v * cols[j + b]
                    i = 3 * a + b
                    sums[i] = p if sums[i] is None else sums[i] + p
        for i in range(9):
            kp[e, pl.ds(i, 1), :] = jnp.sum(sums[i], axis=0, keepdims=True) * grad_scale

    me = 2 * x + c

    def kernel_terms():
        kp[...] = jnp.zeros(kp.shape, F32)
        for e in range(NX * NC):
            kernel_tile(e)
        cps = []
        for i, (dx, dc) in enumerate(squad):
            to = 2 * lax.rem(x + dx, NX) + lax.rem(c + dc, NC)
            cps.append(send(kp.at[to], rk1.at[i], dev(dx=dx, dc=dc)))
        return cps

    def kernel_y(cps):
        for cp in cps:
            cp.wait_recv()
        v = kp[me]
        for i in range(len(squad)):
            v = v + rk1[i]
        rk2[y] = v
        return [send(rk2.at[y], rk2.at[y], dev(dy=d)) for d in range(1, NY)]

    def kernel_z(cps):
        for cp in cps:
            cp.wait_recv()
        rk3[z] = rk2[0] + rk2[1] + rk2[2] + rk2[3]
        return [send(rk3.at[z], rk3.at[z], dev(dz=d)) for d in range(1, NZ)]

    def kernel_all(cps):
        for cp in cps:
            cp.wait_recv()
        v = rk3[0]
        for i in range(1, NZ):
            v = v + rk3[i]
        kf[me] = v
        return [send(kf.at[me], kf.at[me], dev(dx=dx, dc=dc)) for dx, dc in squad]

    def kernel_last(cps):
        for cp in cps:
            cp.wait_recv()
        for e in range(NX * NC):
            for a in range(3):
                for b in range(3):
                    o_gk[a, pl.ds(b, 1), pl.ds(e * 128, 128)] = kf[e, pl.ds(3 * a + b, 1), :]

    def store_in(j, cs, v):
        o_in[j, :, cs] = v

    def store_out(j, v):
        o_out[pl.ds(j * lat, lat), :] = v

    c_b1 = spread1(pb, rb1)
    proc_g(slot3, tok, 0)
    proc_g(slot3, tok, 1)
    back(slot3, tok)
    c_b3 = spread3(pb, rb3)
    transpose(mix, mix_t, 1)
    g2 = weight_grad(2, cot_t, hid)
    g0 = weight_grad(0, mix_t, dg)
    outp(slot3, tok)
    g1 = weight_grad(1, mix_t, du)
    add_core(2, g2)
    zc = z_step(1, None)
    c_b1 += merge(pb, rb3, c_b3, rb1)
    c_o3 = spread3(po, ro3)
    add_core(0, g0)
    y0 = y_first(0)
    c_o1 = spread1(po, ro1)
    zc = z_step(2, zc)
    add_core(1, g1)
    y1 = y_first(1)
    c_o1 += merge(po, ro3, c_o3, ro1)
    total(pb, rb1, c_b1, store_dm)
    c_dh = [send(dm.at[3], dhalo.at[0], lon_up), send(dm.at[0], dhalo.at[1], lon_down)]
    c_k = kernel_terms()
    y0 = y_merge(0, y0)
    zc = z_step(3, zc)
    c_k = kernel_y(c_k)
    for cp in c_dh:
        cp.wait_recv()
    conv(dm, dhalo, True, store_in)
    y1 = y_merge(1, y1)
    zc = z_step(4, zc)
    c_k = kernel_z(c_k)
    z0 = y_last(0, y0)
    c_k = kernel_all(c_k)
    zy = z_done(zc)
    total(po, ro1, c_o1, store_out)
    z1 = y_last(1, y1)
    z_last(0, z0, o_gg)
    kernel_last(c_k)
    zy_last(zy, o_gd)
    z_last(1, z1, o_gu)
    for cp in started:
        cp.wait_send()


def place(*refs):
    for i, (src, dst) in enumerate(zip(refs[:6], refs[6:])):
        dst[...] = jnp.swapaxes(src[...], 0, 1) if i < 2 else src[...]


def shards(fields, conv_kernel, gate_weight, up_weight, down_weight, cotangent):
    _, lat, lon, width = fields.shape
    ff = gate_weight.shape[1]
    tok = lat * lon
    total_tokens = tok * lax.axis_size("shard") * lax.axis_size("lon")
    grad_scale = 1.0 / float(total_tokens) ** 0.5
    rows_d = width // 32
    vmem = lambda *shape, dtype=BF16: pltpu.VMEM(shape, dtype)
    call = pl.pallas_call(
        lambda *refs: kernel(grad_scale, *refs),
        name="swiglu_block",
        out_shape=[
            jax.ShapeDtypeStruct((tok, width), BF16),
            jax.ShapeDtypeStruct((lon, lat, width), BF16),
            jax.ShapeDtypeStruct((rows_d, ff), F32),
            jax.ShapeDtypeStruct((rows_d, ff), F32),
            jax.ShapeDtypeStruct((rows_d, ff), F32),
            jax.ShapeDtypeStruct((3, 3, width), F32),
        ],
        in_specs=[pl.BlockSpec(memory_space=pltpu.VMEM if i == 1 else pl.ANY) for i in range(6)],
        out_specs=[pl.BlockSpec(memory_space=pltpu.VMEM)] * 6,
        scratch_shapes=[
            vmem(lat, lon, width),
            vmem(lat, lon, width),
            vmem(lon, lat, width),
            vmem(width, ff),
            vmem(width, ff),
            vmem(ff, width),
            vmem(2, lat, width),
            vmem(2, lat, width),
            vmem(width, ff),
            vmem(width, ff),
            vmem(ff, width),
            vmem(4 * tok, width),
            vmem(4 * tok, width),
            vmem(4 * tok, 2 * ff),
            vmem(4 * tok, 2 * ff),
            vmem(4 * tok, 2 * ff),
            vmem(4 * tok, width),
            vmem(4 * tok, width),
            vmem(2, tok // 2, width),
            vmem(2, tok, width),
            vmem(2, tok // 2, width),
            vmem(2, tok, width),
            vmem(4 * tok, 2 * ff, dtype=F32),
            vmem(2, width // 2, 4 * tok),
            vmem(2, width // 2, 4 * tok),
            vmem(3, 2, NY, width // 4, ff),
            vmem(3, NY, width // 4, ff),
            vmem(2, 2, width // 8, ff),
            vmem(2, 2, width // 4, ff),
            vmem(2, NZ, 32, ff),
            vmem(2, NZ - 1, 32, ff),
            vmem(2, 4, NY, 32, ff),
            vmem(NY, 32, ff),
            vmem(NY - 1, 32, ff),
            vmem(lon, lat, width),
            vmem(8, 16, width // 8, dtype=F32),
            vmem(7, 16, width // 8, dtype=F32),
            vmem(NY, 16, width // 8, dtype=F32),
            vmem(NZ, 16, width // 8, dtype=F32),
            vmem(8, 16, width // 8, dtype=F32),
            pltpu.SemaphoreType.DMA((N_SEM,)),
            pltpu.SemaphoreType.DMA((N_SEM,)),
            pltpu.SemaphoreType.DMA((5,)),
        ],
        compiler_params=pltpu.CompilerParams(
            collective_id=0, has_side_effects=True, vmem_limit_bytes=60 * 2**20
        ),
        cost_estimate=pl.CostEstimate(flops=14_500_000_000, bytes_accessed=6_000_000, transcendentals=800_000),
    )
    out, in_grad, gg, gu, gd, gk = call(
        fields[0], conv_kernel, gate_weight, up_weight, down_weight, cotangent[0]
    )

    results = (out.reshape(lon, lat, width), in_grad, gg, gu, gd, gk)
    grid_shape = jax.ShapeDtypeStruct((lat, lon, width), BF16)
    out, in_grad, gg, gu, gd, gk = pl.pallas_call(
        place,
        name="place",
        out_shape=[grid_shape] * 2 + [jax.ShapeDtypeStruct(v.shape, v.dtype) for v in results[2:]],
        in_specs=[pl.BlockSpec(memory_space=pltpu.VMEM)] * 6,
        out_specs=[pl.BlockSpec(memory_space=pltpu.VMEM)] * 6,
    )(*results)
    return out[None], in_grad[None], gg, gu, gd.T, gk


def solution(mesh):
    placed = (
        P("shard", None, "lon", None),
        P(),
        P(None, "shard"),
        P(None, "shard"),
        P("shard", None),
        P("shard", None, "lon", None),
    )
    return jax.shard_map(
        shards,
        mesh=mesh,
        in_specs=placed,
        out_specs=(
            P("shard", None, "lon", None),
            P("shard", None, "lon", None),
            P("lon", "shard"),
            P("lon", "shard"),
            P("shard", "lon"),
            P(),
        ),
        check_vma=False,
    )
```

time: 127 us -> 96.3 us (0.76)
  Pallas kernels: 113 us -> 94 us
  local copies, waits for them, and re-layouts: 10.6 us -> 0 us
    pallas_call x1 -> x2, Pallas kernels: 113 us -> 94 us  [the longest x1 91.9 us: shards(): call(fields[0], conv_kernel, gate_weight, up_weight, down_weight, cotange...]
    unnamed x17 -> x0, local copies, waits for them, and re-layouts: 5.53 us -> none
    reshape x3 -> x0, local copies, waits for them, and re-layouts: 4.18 us -> none  [the longest x1 2.1 us: placed(): return v.reshape(lon, lat, width).transpose(1, 0, 2)[None]]
where the time goes in v2:
time: 96.3 us; the launch traced here: 94.7 us
  Pallas kernels  94 us (98%)
    pallas_call x1, Pallas kernels, shards(): call(fields[0], conv_kernel, gate_weight, up_weight, down_weight, cotange...  91.9 us
    pallas_call x1, Pallas kernels, shards(): pl.pallas_call(place, name='place', out_shape=[grid_shape] * 2 + [jax.Sha...  2.17 us

profile of v2, /device:TPU:4, one launch (start us, length us, event | category | flops | bytes accessed | tf_op | source)
XLA Modules:
  0.0 94.7 jit_solution(15170483840245750049)
XLA Ops:
  0.6 91.9 %swiglu_block.1 = (bf16[192,1024]{1,0:T(8,128)(2,1)}, bf16[4,48,1024]{2,1,0:T(8,128)(2,1)}, f32[32,512]{1,0:T(8,128)}, f32[32,512]{1,0:T(8,128)}, f32[32,512]{1,0:T(8,128)}, /*index=5*/f32[3,3,1024]{2,1,0:T(4,128)}) custom-call(bf16[48,4,1024]{2,1,0:T(4,128)(2,1)} %bitcast.7, f32[3,3,1024]{2,1,0:T(4,128)} %refs_1_.1, bf16[1024,512]{1,0:T(8,128)(2,1)} %refs_2_.1, ...), custom_call_target="tpu_custom_call" | custom-call | flops 14499999744 | bytes 6000000 | tf_op jit(solution)/shard_map/swiglu_block/pallas_call | solution.py:546
  92.5 2.2 %place.1 = (bf16[48,4,1024]{2,1,0:T(4,128)(2,1)}, bf16[48,4,1024]{2,1,0:T(4,128)(2,1)}, f32[32,512]{1,0:T(8,128)}, f32[32,512]{1,0:T(8,128)}, f32[32,512]{1,0:T(8,128)}, /*index=5*/f32[3,3,1024]{2,1,0:T(4,128)}) custom-call(bf16[4,48,1024]{2,1,0:T(8,128)(2,1)} %bitcast.6, bf16[4,48,1024]{2,1,0:T(8,128)(2,1)} %get-tuple-element.19.refs_1_, ...), custom_call_target="tpu_custom_call" | custom-call | tf_op jit(solution)/shard_map/place/pallas_call | solution.py:552

commit v3 on v2

--- a/solution.py
+++ b/solution.py
@@ -10,7 +10,7 @@
 NX, NY, NZ, NC = 4, 4, 8, 2
 NN = (((1,), (0,)), ((), ()))
 NT = (((1,), (1,)), ((), ()))
-N_SEM = 128
+N_SEM = 160
 
 
 def mm(a, b, dims=NN):
@@ -35,6 +35,7 @@
     tok = 4 * lat
     half = tok // 2
     ff = wg.shape[1]
+    cols_u = ff // 2
     s, l = lax.axis_index("shard"), lax.axis_index("lon")
     x, yl = lax.rem(s, 4), s // 4
     z, yh, c = l // 4, lax.rem(l // 2, 2), lax.rem(l, 2)
@@ -245,105 +246,103 @@
         b = send(rows(part, slot2 + half, half), near.at[1, pl.ds(half, half)], dev(dx=1))
         return [a, b]
 
-    def weight_grad(g, lhs, rhs):
+    def weight_grad(g, u, lhs, rhs):
         cp = None
         for cc in (1 - c, c):
             for h in range(2):
                 yl2 = yl if h == 0 else 1 - yl
-                v = mm(lhs[cc], rhs[:, pl.ds(h * ff, ff)]) * grad_scale
+                v = mm(lhs[cc], rhs[:, pl.ds(h * ff + u * cols_u, cols_u)]) * grad_scale
                 for yh2 in range(2):
-                    gb[g, cc, yh2 * 2 + yl2] = v[yh2 * 256 : yh2 * 256 + 256].astype(BF16)
+                    gb[g, cc, u, yh2 * 2 + yl2] = v[yh2 * 256 : yh2 * 256 + 256].astype(BF16)
             if cp is None:
-                cp = send(gb.at[g, cc], rc.at[g], dev(dc=1))
+                cp = send(gb.at[g, cc, u], rc.at[g, u], dev(dc=1))
         return cp
 
-    def add_core(g, cp):
+    def add_core(g, u, cp):
         cp.wait_recv()
         for t in range(NY):
-            gb[g, c, t] = (gb[g, c, t].astype(F32) + rc[g, t].astype(F32)).astype(BF16)
+            gb[g, c, u, t] = (gb[g, c, u, t].astype(F32) + rc[g, u, t].astype(F32)).astype(BF16)
 
     yup, ydown, yfar = lax.rem(y + 1, NY), lax.rem(y + 3, NY), lax.rem(y + 2, NY)
-    n_y = gb.shape[3]
-    h_y = n_y // 2
-
-    def y_first(g):
-        lo, hi = pl.ds(0, h_y), pl.ds(h_y, h_y)
+    n_y = gb.shape[4]
+    lo, hi = pl.ds(0, n_y // 2), pl.ds(n_y // 2, n_y // 2)
+
+    def y_first(g, u):
         far = [
-            send(gb.at[g, c, yfar, lo], ry2.at[g, 0], dev(dy=-1)),
-            send(gb.at[g, c, yfar, hi], ry2.at[g, 1], dev(dy=1)),
+            send(gb.at[g, c, u, yfar, lo], ry2.at[g, u, 0], dev(dy=-1)),
+            send(gb.at[g, c, u, yfar, hi], ry2.at[g, u, 1], dev(dy=1)),
         ]
         near = [
-            send(gb.at[g, c, ydown, hi], ry1.at[g, 0, hi], dev(dy=-1)),
-            send(gb.at[g, c, yup, lo], ry1.at[g, 1, lo], dev(dy=1)),
+            send(gb.at[g, c, u, ydown, hi], ry1.at[g, u, 0, hi], dev(dy=-1)),
+            send(gb.at[g, c, u, yup, lo], ry1.at[g, u, 1, lo], dev(dy=1)),
         ]
         return far, near
 
-    def y_merge(g, cps):
+    def y_merge(g, u, cps):
         far, near = cps
-        lo, hi = pl.ds(0, h_y), pl.ds(h_y, h_y)
-        far[0].wait_recv()
-        gb[g, c, ydown, lo] = (gb[g, c, ydown, lo].astype(F32) + ry2[g, 0].astype(F32)).astype(BF16)
-        near.append(send(gb.at[g, c, ydown, lo], ry1.at[g, 0, lo], dev(dy=-1)))
-        far[1].wait_recv()
-        gb[g, c, yup, hi] = (gb[g, c, yup, hi].astype(F32) + ry2[g, 1].astype(F32)).astype(BF16)
-        near.append(send(gb.at[g, c, yup, hi], ry1.at[g, 1, hi], dev(dy=1)))
+        for i, (to, part, sign) in enumerate(((ydown, lo, -1), (yup, hi, 1))):
+            far[i].wait_recv()
+            v = gb[g, c, u, to, part].astype(F32) + ry2[g, u, i].astype(F32)
+            gb[g, c, u, to, part] = v.astype(BF16)
+            near.append(send(gb.at[g, c, u, to, part], ry1.at[g, u, i, part], dev(dy=sign)))
         return near
 
-    def y_last(g, near):
+    def y_last(g, u, near):
         for cp in near:
             cp.wait_recv()
-        v = gb[g, c, y].astype(F32) + ry1[g, 0].astype(F32) + ry1[g, 1].astype(F32)
-        gz[g] = v.astype(BF16).reshape(NZ, 32, ff)
+        v = gb[g, c, u, y].astype(F32) + ry1[g, u, 0].astype(F32) + ry1[g, u, 1].astype(F32)
+        gz[g, u] = v.astype(BF16).reshape(NZ, 32, cols_u)
         return [
-            send(gz.at[g, lax.rem(z + d, NZ)], rz.at[g, d - 1], dev(dz=d))
+            send(gz.at[g, u, lax.rem(z + d, NZ)], rz.at[g, u, d - 1], dev(dz=d))
             for d in (4, 3, 5, 2, 6, 1, 7)
         ]
 
-    def z_last(g, cps, out):
+    def z_last(g, u, cps, out):
         for cp in cps:
             cp.wait_recv()
-        v = gz[g, z].astype(F32)
+        v = gz[g, u, z].astype(F32)
         for d in range(NZ - 1):
-            v = v + rz[g, d].astype(F32)
-        out[...] = v
+            v = v + rz[g, u, d].astype(F32)
+        out[:, pl.ds(u * cols_u, cols_u)] = v
 
     def stripe(d, r0, n):
         return pl.ds(pl.multiple_of(lax.rem(z + d + NZ, NZ) * 32 + r0, 16), n)
 
-    def z_step(k, cps):
+    def z_step(k, u, cps):
         new = []
         for way, sign in ((0, 1), (1, -1)):
             if k == 1:
-                st = stripe(4, way * 16, 16)
-                new.append(send(gb.at[2, c, :, st], zr.at[way, 0, :, pl.ds(way * 16, 16)], dev(dz=sign)))
+                st, r = stripe(4, way * 16, 16), pl.ds(way * 16, 16)
+                new.append(send(gb.at[2, c, u, :, st], zr.at[u, way, 0, :, r], dev(dz=sign)))
                 continue
             cps[way].wait_recv()
             if k == 2:
                 st, r = stripe(3 * sign, way * 16, 16), pl.ds(way * 16, 16)
             else:
                 st, r = stripe((5 - k) * sign, 0, 32), pl.ds(0, 32)
-            gb[2, c, :, st] = (gb[2, c, :, st].astype(F32) + zr[way, k - 2, :, r].astype(F32)).astype(BF16)
+            v = gb[2, c, u, :, st].astype(F32) + zr[u, way, k - 2, :, r].astype(F32)
+            gb[2, c, u, :, st] = v.astype(BF16)
             st = stripe((5 - k) * sign, 0, 32)
-            new.append(send(gb.at[2, c, :, st], zr.at[way, k - 1], dev(dz=sign)))
+            new.append(send(gb.at[2, c, u, :, st], zr.at[u, way, k - 1], dev(dz=sign)))
         return new
 
-    def z_done(cps):
+    def z_done(u, cps):
         for cp in cps:
             cp.wait_recv()
         st = stripe(0, 0, 32)
-        v = gb[2, c, :, st].astype(F32) + zr[0, 3].astype(F32) + zr[1, 3].astype(F32)
-        gy[...] = v.astype(BF16)
+        v = gb[2, c, u, :, st].astype(F32) + zr[u, 0, 3].astype(F32) + zr[u, 1, 3].astype(F32)
+        gy[u] = v.astype(BF16)
         return [
-            send(gy.at[lax.rem(y + d, NY)], rzy.at[d - 1], dev(dy=d)) for d in range(1, NY)
+            send(gy.at[u, lax.rem(y + d, NY)], rzy.at[u, d - 1], dev(dy=d)) for d in range(1, NY)
         ]
 
-    def zy_last(cps, out):
+    def zy_last(u, cps, out):
         for cp in cps:
             cp.wait_recv()
-        v = gy[y].astype(F32)
+        v = gy[u, y].astype(F32)
         for d in range(NY - 1):
-            v = v + rzy[d].astype(F32)
-        out[...] = v
+            v = v + rzy[u, d].astype(F32)
+        out[:, pl.ds(u * cols_u, cols_u)] = v
 
     def total(part, near, copies, store):
         for cp in copies:
@@ -427,42 +426,62 @@
     back(slot3, tok)
     c_b3 = spread3(pb, rb3)
     transpose(mix, mix_t, 1)
-    g2 = weight_grad(2, cot_t, hid)
-    g0 = weight_grad(0, mix_t, dg)
+    g00 = weight_grad(0, 0, mix_t, dg)
+    g20 = weight_grad(2, 0, cot_t, hid)
+    g01 = weight_grad(0, 1, mix_t, dg)
+    add_core(0, 0, g00)
+    y00 = y_first(0, 0)
+    g21 = weight_grad(2, 1, cot_t, hid)
+    add_core(2, 0, g20)
+    za = z_step(1, 0, None)
+    g10 = weight_grad(1, 0, mix_t, du)
+    add_core(0, 1, g01)
+    y01 = y_first(0, 1)
+    g11 = weight_grad(1, 1, mix_t, du)
+    c_b1 += merge(pb, rb3, c_b3, rb1)
+    add_core(2, 1, g21)
+    zb = z_step(1, 1, None)
+    y00 = y_merge(0, 0, y00)
+    za = z_step(2, 0, za)
     outp(slot3, tok)
-    g1 = weight_grad(1, mix_t, du)
-    add_core(2, g2)
-    zc = z_step(1, None)
-    c_b1 += merge(pb, rb3, c_b3, rb1)
     c_o3 = spread3(po, ro3)
-    add_core(0, g0)
-    y0 = y_first(0)
+    add_core(1, 0, g10)
+    y10 = y_first(1, 0)
+    zb = z_step(2, 1, zb)
+    add_core(1, 1, g11)
+    y11 = y_first(1, 1)
     c_o1 = spread1(po, ro1)
-    zc = z_step(2, zc)
-    add_core(1, g1)
-    y1 = y_first(1)
-    c_o1 += merge(po, ro3, c_o3, ro1)
+    y01 = y_merge(0, 1, y01)
+    za = z_step(3, 0, za)
     total(pb, rb1, c_b1, store_dm)
     c_dh = [send(dm.at[3], dhalo.at[0], lon_up), send(dm.at[0], dhalo.at[1], lon_down)]
     c_k = kernel_terms()
-    y0 = y_merge(0, y0)
-    zc = z_step(3, zc)
+    y00 = y_last(0, 0, y00)
+    zb = z_step(3, 1, zb)
+    y10 = y_merge(1, 0, y10)
+    za = z_step(4, 0, za)
     c_k = kernel_y(c_k)
+    y11 = y_merge(1, 1, y11)
+    y01 = y_last(0, 1, y01)
+    zb = z_step(4, 1, zb)
+    c_o1 += merge(po, ro3, c_o3, ro1)
+    c_k = kernel_z(c_k)
     for cp in c_dh:
         cp.wait_recv()
     conv(dm, dhalo, True, store_in)
-    y1 = y_merge(1, y1)
-    zc = z_step(4, zc)
-    c_k = kernel_z(c_k)
-    z0 = y_last(0, y0)
+    za = z_done(0, za)
+    y10 = y_last(1, 0, y10)
     c_k = kernel_all(c_k)
-    zy = z_done(zc)
+    y11 = y_last(1, 1, y11)
+    zb = z_done(1, zb)
+    z_last(0, 0, y00, o_gg)
+    z_last(0, 1, y01, o_gg)
     total(po, ro1, c_o1, store_out)
-    z1 = y_last(1, y1)
-    z_last(0, z0, o_gg)
     kernel_last(c_k)
-    zy_last(zy, o_gd)
-    z_last(1, z1, o_gu)
+    zy_last(0, za, o_gd)
+    z_last(1, 0, y10, o_gu)
+    zy_last(1, zb, o_gd)
+    z_last(1, 1, y11, o_gu)
     for cp in started:
         cp.wait_send()
 
@@ -519,15 +538,15 @@
             vmem(4 * tok, 2 * ff, dtype=F32),
             vmem(2, width // 2, 4 * tok),
             vmem(2, width // 2, 4 * tok),
-            vmem(3, 2, NY, width // 4, ff),
-            vmem(3, NY, width // 4, ff),
-            vmem(2, 2, width // 8, ff),
-            vmem(2, 2, width // 4, ff),
-            vmem(2, NZ, 32, ff),
-            vmem(2, NZ - 1, 32, ff),
-            vmem(2, 4, NY, 32, ff),
-            vmem(NY, 32, ff),
-            vmem(NY - 1, 32, ff),
+            vmem(3, 2, 2, NY, width // 4, ff // 2),
+            vmem(3, 2, NY, width // 4, ff // 2),
+            vmem(2, 2, 2, width // 8, ff // 2),
+            vmem(2, 2, 2, width // 4, ff // 2),
+            vmem(2, 2, NZ, 32, ff // 2),
+            vmem(2, 2, NZ - 1, 32, ff // 2),
+            vmem(2, 2, 4, NY, 32, ff // 2),
+            vmem(2, NY, 32, ff // 2),
+            vmem(2, NY - 1, 32, ff // 2),
             vmem(lon, lat, width),
             vmem(8, 16, width // 8, dtype=F32),
             vmem(7, 16, width // 8, dtype=F32),

time: 96.3 us -> 89.1 us (0.925); the launches traced: 94.7 us -> 88.7 us
  Pallas kernels: 94 us -> 88 us
    pallas_call x1, Pallas kernels: 91.9 us -> 85.8 us  [shards(): call(fields[0], conv_kernel, gate_weight, up_weight, down_weight, cotange...]
where the time goes in v3:
time: 89.1 us; the launch traced here: 88.7 us
  Pallas kernels  88 us (99%)
    pallas_call x1, Pallas kernels, shards(): call(fields[0], conv_kernel, gate_weight, up_weight, down_weight, cotange...  85.8 us
    pallas_call x1, Pallas kernels, shards(): pl.pallas_call(place, name='place', out_shape=[grid_shape] * 2 + [jax.Sha...  2.17 us

profile of v3, /device:TPU:4, one launch (start us, length us, event | category | flops | bytes accessed | tf_op | source)
XLA Modules:
  0.0 88.7 jit_solution(16534122713847290040)
XLA Ops:
  0.6 85.8 %swiglu_block.1 = (bf16[192,1024]{1,0:T(8,128)(2,1)}, bf16[4,48,1024]{2,1,0:T(8,128)(2,1)}, f32[32,512]{1,0:T(8,128)}, f32[32,512]{1,0:T(8,128)}, f32[32,512]{1,0:T(8,128)}, /*index=5*/f32[3,3,1024]{2,1,0:T(4,128)}) custom-call(bf16[48,4,1024]{2,1,0:T(4,128)(2,1)} %bitcast.7, f32[3,3,1024]{2,1,0:T(4,128)} %refs_1_.1, bf16[1024,512]{1,0:T(8,128)(2,1)} %refs_2_.1, ...), custom_call_target="tpu_custom_call" | custom-call | flops 14499999744 | bytes 6000000 | tf_op jit(solution)/shard_map/swiglu_block/pallas_call | solution.py:565
  86.5 2.2 %place.1 = (bf16[48,4,1024]{2,1,0:T(4,128)(2,1)}, bf16[48,4,1024]{2,1,0:T(4,128)(2,1)}, f32[32,512]{1,0:T(8,128)}, f32[32,512]{1,0:T(8,128)}, f32[32,512]{1,0:T(8,128)}, /*index=5*/f32[3,3,1024]{2,1,0:T(4,128)}) custom-call(bf16[4,48,1024]{2,1,0:T(8,128)(2,1)} %bitcast.6, bf16[4,48,1024]{2,1,0:T(8,128)(2,1)} %get-tuple-element.19.refs_1_, ...), custom_call_target="tpu_custom_call" | custom-call | tf_op jit(solution)/shard_map/place/pallas_call | solution.py:571

commit v4 on v3

--- a/solution.py
+++ b/solution.py
@@ -19,7 +19,8 @@
 
 def kernel(
     grad_scale, f_in, k_ref, wg_in, wu_in, wd_in, t_in,
-    o_out, o_in, o_gg, o_gu, o_gd, o_gk,
+    h_out, h_in, h_gg, h_gu, h_gd, h_gk,
+    o_out, o_in, o_gg, o_gu, o_gd, o_gk, tmp,
     f_raw, t_raw, f_ref, wg, wu, wd, halo, dhalo, wg2, wu2, wd2, mix, cot, hid, dg, du, pb, po, rb3, rb1, ro3, ro1,
     dh, mix_t, cot_t, gb, rc, ry2, ry1, gz, rz, zr, gy, rzy, dm, kp, rk1, rk2, rk3, kf, ssem, rsem, lsem,
 ):
@@ -27,7 +28,7 @@
     local = [
         pltpu.make_async_copy(src, dst, lsem.at[i])
         for i, (src, dst) in enumerate((
-            (f_in, f_raw), (t_in, t_raw), (wd_in, wd), (wg_in, wg), (wu_in, wu),
+            (t_in, t_raw), (f_in, f_raw), (wd_in, wd), (wg_in, wg), (wu_in, wu),
         ))
     ]
     for cp in local:
@@ -59,6 +60,8 @@
     barrier = pltpu.get_barrier_semaphore()
     for p in partners:
         pl.semaphore_signal(barrier, inc=1, device_id=p, device_id_type=MESH)
+    local[0].wait()
+    cot[pl.ds(0, tok), :] = jnp.swapaxes(t_raw[...], 0, 1).reshape(tok, width)
     pl.semaphore_wait(barrier, len(partners))
 
     started = []
@@ -76,16 +79,14 @@
     def rows(ref, r0, n):
         return ref.at[pl.ds(r0, n)]
 
-    local[0].wait()
-    f_ref[...] = jnp.swapaxes(f_raw[...], 0, 1)
-    c_halo = [send(f_ref.at[3], halo.at[0], lon_up), send(f_ref.at[0], halo.at[1], lon_down)]
     slot1, slot2, slot3 = tok, 2 * tok, 3 * tok
-    local[1].wait()
-    cot[pl.ds(0, tok), :] = jnp.swapaxes(t_raw[...], 0, 1).reshape(tok, width)
     c_cot = [
         send(rows(cot, 0, tok), rows(cot, slot1, tok), dev(dx=1)),
         send(rows(cot, 0, tok), rows(cot, slot2, tok), dev(dx=-1)),
     ]
+    local[1].wait()
+    f_ref[...] = jnp.swapaxes(f_raw[...], 0, 1)
+    c_halo = [send(f_ref.at[3], halo.at[0], lon_up), send(f_ref.at[0], halo.at[1], lon_down)]
     c_w = []
     for i, (own, other) in enumerate(((wd, wd2), (wg, wg2), (wu, wu2))):
         local[2 + i].wait()
@@ -344,6 +345,13 @@
             v = v + rzy[u, d].astype(F32)
         out[:, pl.ds(u * cols_u, cols_u)] = v
 
+    leaving = []
+
+    def leave(src, dst):
+        cp = pltpu.make_async_copy(src, dst, lsem.at[5 + len(leaving)])
+        cp.start()
+        leaving.append(cp)
+
     def total(part, near, copies, store):
         for cp in copies:
             cp.wait_recv()
@@ -415,10 +423,10 @@
                     o_gk[a, pl.ds(b, 1), pl.ds(e * 128, 128)] = kf[e, pl.ds(3 * a + b, 1), :]
 
     def store_in(j, cs, v):
-        o_in[j, :, cs] = v
+        tmp[j, :, cs] = v
 
     def store_out(j, v):
-        o_out[pl.ds(j * lat, lat), :] = v
+        tmp[j] = v
 
     c_b1 = spread1(pb, rb1)
     proc_g(slot3, tok, 0)
@@ -444,51 +452,61 @@
     y00 = y_merge(0, 0, y00)
     za = z_step(2, 0, za)
     outp(slot3, tok)
-    c_o3 = spread3(po, ro3)
     add_core(1, 0, g10)
     y10 = y_first(1, 0)
     zb = z_step(2, 1, zb)
     add_core(1, 1, g11)
     y11 = y_first(1, 1)
-    c_o1 = spread1(po, ro1)
     y01 = y_merge(0, 1, y01)
     za = z_step(3, 0, za)
     total(pb, rb1, c_b1, store_dm)
     c_dh = [send(dm.at[3], dhalo.at[0], lon_up), send(dm.at[0], dhalo.at[1], lon_down)]
     c_k = kernel_terms()
+    c_o3 = spread3(po, ro3)
+    c_o1 = spread1(po, ro1)
     y00 = y_last(0, 0, y00)
+    c_k = kernel_y(c_k)
     zb = z_step(3, 1, zb)
     y10 = y_merge(1, 0, y10)
     za = z_step(4, 0, za)
-    c_k = kernel_y(c_k)
+    c_k = kernel_z(c_k)
     y11 = y_merge(1, 1, y11)
     y01 = y_last(0, 1, y01)
+    c_k = kernel_all(c_k)
     zb = z_step(4, 1, zb)
     c_o1 += merge(po, ro3, c_o3, ro1)
-    c_k = kernel_z(c_k)
     for cp in c_dh:
         cp.wait_recv()
     conv(dm, dhalo, True, store_in)
+    o_in[...] = jnp.swapaxes(tmp[...], 0, 1)
+    leave(o_in, h_in)
     za = z_done(0, za)
     y10 = y_last(1, 0, y10)
-    c_k = kernel_all(c_k)
     y11 = y_last(1, 1, y11)
     zb = z_done(1, zb)
     z_last(0, 0, y00, o_gg)
     z_last(0, 1, y01, o_gg)
+    leave(o_gg, h_gg)
     total(po, ro1, c_o1, store_out)
+    o_out[...] = jnp.swapaxes(tmp[...], 0, 1)
+    leave(o_out, h_out)
     kernel_last(c_k)
+    leave(o_gk, h_gk)
     zy_last(0, za, o_gd)
+    zy_last(1, zb, o_gd)
+    leave(o_gd, h_gd)
     z_last(1, 0, y10, o_gu)
-    zy_last(1, zb, o_gd)
     z_last(1, 1, y11, o_gu)
+    leave(o_gu, h_gu)
     for cp in started:
         cp.wait_send()
+    for cp in leaving:
+        cp.wait()
 
 
 def place(*refs):
-    for i, (src, dst) in enumerate(zip(refs[:6], refs[6:])):
-        dst[...] = jnp.swapaxes(src[...], 0, 1) if i < 2 else src[...]
+    for src, dst in zip(refs[:6], refs[6:]):
+        dst[...] = src[...]
 
 
 def shards(fields, conv_kernel, gate_weight, up_weight, down_weight, cotangent):
@@ -503,16 +521,23 @@
         lambda *refs: kernel(grad_scale, *refs),
         name="swiglu_block",
         out_shape=[
-            jax.ShapeDtypeStruct((tok, width), BF16),
-            jax.ShapeDtypeStruct((lon, lat, width), BF16),
+            jax.ShapeDtypeStruct((lat, lon, width), BF16),
+            jax.ShapeDtypeStruct((lat, lon, width), BF16),
             jax.ShapeDtypeStruct((rows_d, ff), F32),
             jax.ShapeDtypeStruct((rows_d, ff), F32),
             jax.ShapeDtypeStruct((rows_d, ff), F32),
             jax.ShapeDtypeStruct((3, 3, width), F32),
         ],
         in_specs=[pl.BlockSpec(memory_space=pltpu.VMEM if i == 1 else pl.ANY) for i in range(6)],
-        out_specs=[pl.BlockSpec(memory_space=pltpu.VMEM)] * 6,
+        out_specs=[pl.BlockSpec(memory_space=pl.ANY)] * 6,
         scratch_shapes=[
+            vmem(lat, lon, width),
+            vmem(lat, lon, width),
+            vmem(rows_d, ff, dtype=F32),
+            vmem(rows_d, ff, dtype=F32),
+            vmem(rows_d, ff, dtype=F32),
+            vmem(3, 3, width, dtype=F32),
+            vmem(lon, lat, width),
             vmem(lat, lon, width),
             vmem(lat, lon, width),
             vmem(lon, lat, width),
@@ -555,7 +580,7 @@
             vmem(8, 16, width // 8, dtype=F32),
             pltpu.SemaphoreType.DMA((N_SEM,)),
             pltpu.SemaphoreType.DMA((N_SEM,)),
-            pltpu.SemaphoreType.DMA((5,)),
+            pltpu.SemaphoreType.DMA((11,)),
         ],
         compiler_params=pltpu.CompilerParams(
             collective_id=0, has_side_effects=True, vmem_limit_bytes=60 * 2**20
@@ -566,12 +591,11 @@
         fields[0], conv_kernel, gate_weight, up_weight, down_weight, cotangent[0]
     )
 
-    results = (out.reshape(lon, lat, width), in_grad, gg, gu, gd, gk)
-    grid_shape = jax.ShapeDtypeStruct((lat, lon, width), BF16)
+    results = (out, in_grad, gg, gu, gd, gk)
     out, in_grad, gg, gu, gd, gk = pl.pallas_call(
         place,
         name="place",
-        out_shape=[grid_shape] * 2 + [jax.ShapeDtypeStruct(v.shape, v.dtype) for v in results[2:]],
+        out_shape=[jax.ShapeDtypeStruct(v.shape, v.dtype) for v in results],
         in_specs=[pl.BlockSpec(memory_space=pltpu.VMEM)] * 6,
         out_specs=[pl.BlockSpec(memory_space=pltpu.VMEM)] * 6,
     )(*results)

time: 89.1 us -> 85.4 us (0.958)
  Pallas kernels: 88 us -> 84.6 us
    pallas_call x1, Pallas kernels: 85.8 us -> 82.5 us  [shards(): call(fields[0], conv_kernel, gate_weight, up_weight, down_weight, cotange...]
where the time goes in v4:
time: 85.4 us; the launch traced here: 85.3 us
  Pallas kernels  84.6 us (99%)
    pallas_call x1, Pallas kernels, shards(): call(fields[0], conv_kernel, gate_weight, up_weight, down_weight, cotange...  82.5 us
    pallas_call x1, Pallas kernels, shards(): pl.pallas_call(place, name='place', out_shape=[jax.ShapeDtypeStruct(v.sha...  2.13 us

profile of v4, /device:TPU:4, one launch (start us, length us, event | category | flops | bytes accessed | tf_op | source)
XLA Modules:
  0.0 85.3 jit_solution(1897969130869567968)
XLA Ops:
  0.6 82.5 %swiglu_block.1 = (bf16[48,4,1024]{2,1,0:T(4,128)(2,1)}, bf16[48,4,1024]{2,1,0:T(4,128)(2,1)}, f32[32,512]{1,0:T(8,128)}, f32[32,512]{1,0:T(8,128)}, f32[32,512]{1,0:T(8,128)}, /*index=5*/f32[3,3,1024]{2,1,0:T(4,128)}) custom-call(bf16[48,4,1024]{2,1,0:T(4,128)(2,1)} %bitcast.5, f32[3,3,1024]{2,1,0:T(4,128)} %refs_1_.1, bf16[1024,512]{1,0:T(8,128)(2,1)} %refs_2_.1, ...), custom_call_target="tpu_custom_call" | custom-call | flops 14499999744 | bytes 6000000 | tf_op jit(solution)/shard_map/swiglu_block/pallas_call | solution.py:590
  83.1 2.1 %place.1 = (bf16[48,4,1024]{2,1,0:T(4,128)(2,1)}, bf16[48,4,1024]{2,1,0:T(4,128)(2,1)}, f32[32,512]{1,0:T(8,128)}, f32[32,512]{1,0:T(8,128)}, f32[32,512]{1,0:T(8,128)}, /*index=5*/f32[3,3,1024]{2,1,0:T(4,128)}) custom-call(bf16[48,4,1024]{2,1,0:T(4,128)(2,1)} %get-tuple-element.18.refs_0_, bf16[48,4,1024]{2,1,0:T(4,128)(2,1)} %get-tuple-element.19.refs_1_, ...), custom_call_target="tpu_custom_call" | custom-call | tf_op jit(solution)/shard_map/place/pallas_call | solution.py:595
